TPU v7x, 512 devices: a whole 4x4x16 slice. The times are simulated.
512 devices in a mesh: gx: 16 (over z), gy: 8 (over x, core), gz: 4 (over y).
Axes of the slice: x: 4, y: 4, z: 16, core: 2. Of those that a mesh axis runs over, the one named last changes fastest.
Arguments:
- fluid_adjoint: float32 [128, 128, 512], P('gx', 'gy', 'gz'), may hold values from -6 to 6
- fluid_source: float32 [128, 128, 512], P('gx', 'gy', 'gz'), may hold values from -6 to 6
- inverse_x: float32 [128, 8], P('gx')
- inverse_y: float32 [128, 16], P('gy')
- inverse_z: float32 [512, 128], P('gz')
- face_cells: int32 [262144, 4], P(('gx', 'gy', 'gz')), may hold values from 0 to 16383
- face_weight: float32 [262144, 4], P(('gx', 'gy', 'gz')), may hold values from 0.1 to 1
- face_owner: int32 [262144, 1], P(('gx', 'gy', 'gz')), may hold values from 0 to 31; in each aligned block of 512 rows (0 to 511, 512 to 1023, ...) at most 40 rows name the same one
- face_solid: int32 [262144], P(('gx', 'gy', 'gz')), may hold values from 0 to 511
- solid_inverse: float32 [262144, 512], P(('gx', 'gy', 'gz'))
- solid_source: float32 [262144], P(('gx', 'gy', 'gz')), may hold values from -6 to 6
Outputs:
- fluid_result: float32 [128, 128, 512], P('gx', 'gy', 'gz')
- solid_adjoint: float32 [262144], P(('gx', 'gy', 'gz'))
Inputs may be any that keep to these rules, and one draw needn't show every extreme that they name: `face_owner`: within the faces of one fluid device, no owner is named by more than 40 faces, a bound that some block reaches.
All inputs are finite; a program needn't handle non-finite values.
Results may differ from a plain program's by a relative error of at most 0.0001.
Values sent between devices are 32-bit elements; how exact they have to be, the bound alone decides.
No kernel may reach another device: no remote copies, remote signals or barrier semaphores. Data moves between devices by JAX's collectives and lax.ppermute only.
A program may use at most 64 MiB of HBM per device.

v0:
```python
import jax
import jax.numpy as jnp
from jax import lax
from jax.sharding import PartitionSpec as P

SWEEPS = 8


RELAX = 0.15
SPREAD = 0.06
COUPLE = 0.5
FORMS = ("jab,ji->iab", "ajb,ji->aib", "abj,ji->abi")


def padded_2(shard, sides, width):
    for axis, dim in sides:
        count, length = (lax.axis_size(axis), shard.shape[dim])
        up = [(i, (i + 1) % count) for i in range(count - 1)]
        down = [(j, i) for i, j in up]
        last = lax.slice_in_dim(shard, length - width, length, axis=dim)
        initial = lax.slice_in_dim(shard, 0, width, axis=dim)
        before = lax.ppermute(last, axis, up)
        after = lax.ppermute(initial, axis, down)
        shard = jnp.concatenate([before, shard, after], axis=dim)
    return shard


def stencil(extended, along, length):
    pieces = [
        lax.slice_in_dim(extended, offset, offset + length, axis=along) for offset in range(5)
    ]
    return (16.0 * (pieces[1] + pieces[3]) - 30.0 * pieces[2] - pieces[0] - pieces[4]) / 12.0


def block_apply(matrix, operand, along):
    return jnp.einsum(FORMS[along], operand, matrix, precision=lax.Precision.HIGHEST)


def gather_rims(adjoint):
    padded = padded_2(adjoint, (("gx", 0), ("gy", 1), ("gz", 2)), 2)
    lowers = (padded[0:2, 2:-2, 2:-2], padded[2:-2, 0:2, 2:-2], padded[2:-2, 2:-2, 0:2])
    uppers = (padded[-2:, 2:-2, 2:-2], padded[2:-2, -2:, 2:-2], padded[2:-2, 2:-2, -2:])
    return (lowers, uppers)


def direction_term(matrix, adjoint, lower, upper, along):
    length = adjoint.shape[along]
    extended = jnp.concatenate([lower, adjoint, upper], axis=along)
    return block_apply(matrix, stencil(extended, along, length), along)


def shards(
    fluid_adjoint,
    fluid_source,
    inverse_x,
    inverse_y,
    inverse_z,
    face_cells,
    face_weight,
    face_owner,
    face_solid,
    solid_inverse,
    solid_source,
):
    size_y = lax.axis_size("gy")
    size_z = lax.axis_size("gz")
    owners = size_y * size_z
    face_count = face_owner.shape[0]
    capacity = max(2, 5 * face_count // (2 * owners))
    flat_cells = fluid_adjoint.reshape(-1)
    flux = jnp.sum(face_weight * flat_cells[face_cells], axis=1)
    target_owner = face_owner[:, 0]
    matches = (target_owner[:, None] == jnp.arange(owners, dtype=jnp.int32)[None, :]).astype(
        jnp.int32
    )
    slot_index = jnp.sum((jnp.cumsum(matches, axis=0) - 1) * matches, axis=1)
    position = target_owner * capacity + slot_index
    send_flux = jnp.zeros((owners * capacity,), jnp.float32).at[position].set(flux)
    send_cells = jnp.zeros((owners * capacity,), jnp.int32).at[position].set(face_solid)
    arrived_flux, arrived_cells = (
        lax.all_to_all(
            send_flux.reshape(owners, capacity),
            ("gy", "gz"),
            split_axis=0,
            concat_axis=0,
            tiled=True,
        ),
        lax.all_to_all(
            send_cells.reshape(owners, capacity),
            ("gy", "gz"),
            split_axis=0,
            concat_axis=0,
            tiled=True,
        ),
    )
    arrived_cells = arrived_cells.reshape(-1)
    heat = solid_source + jnp.zeros(solid_source.shape, jnp.float32).at[arrived_cells].add(
        arrived_flux.reshape(-1)
    )
    solid_result = jnp.dot(solid_inverse.T, heat, precision=lax.Precision.HIGHEST)
    returned = solid_result[arrived_cells]
    face_values = lax.all_to_all(
        returned.reshape(owners, capacity), ("gy", "gz"), split_axis=0, concat_axis=0, tiled=True
    )
    face_temp = face_values.reshape(-1)[position]
    coupled = (
        jnp.zeros(flat_cells.shape, jnp.float32)
        .at[face_cells.reshape(-1)]
        .add((face_weight * face_temp[:, None]).reshape(-1))
    )
    adjoint = fluid_adjoint
    for sweep in range(SWEEPS):
        lowers, uppers = gather_rims(adjoint)
        total = direction_term(inverse_x, adjoint, lowers[0], uppers[0], 0)
        total = total + direction_term(inverse_y, adjoint, lowers[1], uppers[1], 1)
        total = total + direction_term(inverse_z, adjoint, lowers[2], uppers[2], 2)
        adjoint = adjoint + RELAX * (fluid_source - adjoint) + SPREAD * total
    return (adjoint + COUPLE * coupled.reshape(adjoint.shape), solid_result)


def solution(mesh):
    in_specs = (
        P("gx", "gy", "gz"),
        P("gx", "gy", "gz"),
        P("gx", None),
        P("gy", None),
        P("gz", None),
        P(("gx", "gy", "gz"), None),
        P(("gx", "gy", "gz"), None),
        P(("gx", "gy", "gz"), None),
        P(("gx", "gy", "gz")),
        P(("gx", "gy", "gz"), None),
        P(("gx", "gy", "gz")),
    )
    out_specs = (P("gx", "gy", "gz"), P(("gx", "gy", "gz")))
    return jax.shard_map(shards, mesh=mesh, in_specs=in_specs, out_specs=out_specs, check_vma=False)
```

profile of v0, /device:TPU:1, one launch (start us, length us, event | category | flops | bytes accessed | tf_op | source)
XLA Modules:
  0.0 290.7 jit_solution(17782979268318084676)
XLA Ops:
  1.6 4.4 %collective-permute-start = (f32[2,16,128]{2,0,1:T(2,128)S(1)}, f32[2,16,128]{2,0,1:T(2,128)S(1)}, u32[]{:S(2)}, u32[]{:S(2)}) collective-permute-start(f32[2,16,128]{2,0,1:T(2,128)S(1)} %get-tuple-element.53), channel_id=1, source_target_pairs={{0,32},{32,64},{64,96},{96,128},{128,160},{160,192},{192,224},{224... | collective-permute-start | bytes 49160 | tf_op jit(solution)/shard_map/ppermute | solution.py:22
  10.7 4.9 %collective-permute-start.2 = (f32[12,2,128]{2,0,1:T(8,128)S(1)}, f32[12,2,128]{2,0,1:T(8,128)S(1)}, u32[]{:S(2)}, u32[]{:S(2)}) collective-permute-start(f32[12,2,128]{2,0,1:T(8,128)S(1)} %get-tuple-element.36), channel_id=1, source_target_pairs={{0,4},{4,8},{8,12},{12,16},{16,20},{20,24},{24,28},{1,5},{5,9},{9,... | collective-permute-start | bytes 36872 | tf_op jit(solution)/shard_map/ppermute | solution.py:22
  40.7 5.2 %collective-permute-start.8 = (f32[12,2,128]{2,0,1:T(8,128)S(1)}, f32[12,2,128]{2,0,1:T(8,128)S(1)}, u32[]{:S(2)}, u32[]{:S(2)}) collective-permute-start(f32[12,2,128]{2,0,1:T(8,128)S(1)} %get-tuple-element.34), channel_id=1, source_target_pairs={{0,4},{4,8},{8,12},{12,16},{16,20},{20,24},{24,28},{1,5},{5,9},{9,... | collective-permute-start | bytes 36872 | tf_op jit(solution)/shard_map/ppermute | solution.py:22
  56.7 4.1 %collective-permute-done.11 = f32[12,20,2]{2,0,1:T(8,128)S(1)} collective-permute-done((f32[12,20,2]{2,0,1:T(8,128)S(1)}, f32[12,20,2]{2,0,1:T(8,128)S(1)}, u32[]{:S(2)}, u32[]{:S(2)}) %collective-permute-start.11) | collective-permute-done | bytes 1952 | tf_op jit(solution)/shard_map/ppermute | solution.py:23
  61.2 4.8 %collective-permute-start.12 = (f32[2,16,128]{2,0,1:T(2,128)S(1)}, f32[2,16,128]{2,0,1:T(2,128)S(1)}, u32[]{:S(2)}, u32[]{:S(2)}) collective-permute-start(f32[2,16,128]{2,0,1:T(2,128)S(1)} %get-tuple-element.48), channel_id=1, source_target_pairs={{0,32},{32,64},{64,96},{96,128},{128,160},{160,192},{192,224},{224... | collective-permute-start | bytes 49160 | tf_op jit(solution)/shard_map/ppermute | solution.py:22
  71.1 4.9 %collective-permute-start.14 = (f32[12,2,128]{2,0,1:T(8,128)S(1)}, f32[12,2,128]{2,0,1:T(8,128)S(1)}, u32[]{:S(2)}, u32[]{:S(2)}) collective-permute-start(f32[12,2,128]{2,0,1:T(8,128)S(1)} %get-tuple-element.32), channel_id=1, source_target_pairs={{0,4},{4,8},{8,12},{12,16},{16,20},{20,24},{24,28},{1,5},{5,9},{9,... | collective-permute-start | bytes 36872 | tf_op jit(solution)/shard_map/ppermute | solution.py:22
  81.3 5.5 %all-to-all-start = ((s32[32,1,40]{2,1,0:T(1,128)}), s32[32,1,40]{2,1,0:T(1,128)S(1)}, u32[]{:S(2)}, u32[]{:S(2)}) async-start(s32[32,1,40]{2,1,0:T(1,128)} %all_to_all.18), calls=%async_computation | async-start | bytes 32768 | tf_op jit(solution)/shard_map/all_to_all | solution.py:88
  106.3 5.7 %collective-permute-start.20 = (f32[12,2,128]{2,0,1:T(8,128)S(1)}, f32[12,2,128]{2,0,1:T(8,128)S(1)}, u32[]{:S(2)}, u32[]{:S(2)}) collective-permute-start(f32[12,2,128]{2,0,1:T(8,128)S(1)} %get-tuple-element.30), channel_id=1, source_target_pairs={{0,4},{4,8},{8,12},{12,16},{16,20},{20,24},{24,28},{1,5},{5,9},{9,... | collective-permute-start | bytes 36872 | tf_op jit(solution)/shard_map/ppermute | solution.py:22
  122.8 4.1 %collective-permute-done.23 = f32[12,20,2]{2,0,1:T(8,128)S(1)} collective-permute-done((f32[12,20,2]{2,0,1:T(8,128)S(1)}, f32[12,20,2]{2,0,1:T(8,128)S(1)}, u32[]{:S(2)}, u32[]{:S(2)}) %collective-permute-start.23) | collective-permute-done | bytes 1952 | tf_op jit(solution)/shard_map/ppermute | solution.py:23
  127.4 4.5 %collective-permute-start.24 = (f32[2,16,128]{2,0,1:T(2,128)S(1)}, f32[2,16,128]{2,0,1:T(2,128)S(1)}, u32[]{:S(2)}, u32[]{:S(2)}) collective-permute-start(f32[2,16,128]{2,0,1:T(2,128)S(1)} %get-tuple-element.44), channel_id=1, source_target_pairs={{0,32},{32,64},{64,96},{96,128},{128,160},{160,192},{192,224},{224... | collective-permute-start | bytes 49160 | tf_op jit(solution)/shard_map/ppermute | solution.py:22
  133.1 11.8 %gather_fusion = f32[2048]{0:T(1024)S(1)} fusion(f32[16384]{0:T(1024)S(1)} %bitcast.141, s32[2048]{0:T(1024)S(1)} %broadcast_clamp_fusion), kind=kCustom, calls=%fused_computation | custom fusion | bytes 24576 | tf_op jit(solution)/shard_map/gather | solution.py:71
  145.8 4.6 %collective-permute-start.26 = (f32[12,2,128]{2,0,1:T(8,128)S(1)}, f32[12,2,128]{2,0,1:T(8,128)S(1)}, u32[]{:S(2)}, u32[]{:S(2)}) collective-permute-start(f32[12,2,128]{2,0,1:T(8,128)S(1)} %get-tuple-element.28), channel_id=1, source_target_pairs={{0,4},{4,8},{8,12},{12,16},{16,20},{20,24},{24,28},{1,5},{5,9},{9,... | collective-permute-start | bytes 36872 | tf_op jit(solution)/shard_map/ppermute | solution.py:22
  155.6 5.9 %all-to-all-start.1 = ((f32[32,1,40]{2,1,0:T(1,128)}), f32[32,1,40]{2,1,0:T(1,128)S(1)}, u32[]{:S(2)}, u32[]{:S(2)}) async-start(f32[32,1,40]{2,1,0:T(1,128)} %all_to_all.20), calls=%async_computation.1 | async-start | bytes 32768 | tf_op jit(solution)/shard_map/all_to_all | solution.py:81
  173.7 4.3 %collective-permute-start.30 = (f32[2,16,128]{2,0,1:T(2,128)S(1)}, f32[2,16,128]{2,0,1:T(2,128)S(1)}, u32[]{:S(2)}, u32[]{:S(2)}) collective-permute-start(f32[2,16,128]{2,0,1:T(2,128)S(1)} %get-tuple-element.42), channel_id=1, source_target_pairs={{0,32},{32,64},{64,96},{96,128},{128,160},{160,192},{192,224},{224... | collective-permute-start | bytes 49160 | tf_op jit(solution)/shard_map/ppermute | solution.py:22
  180.8 9.4 %scatter_fusion = f32[512]{0:T(512)S(1)} fusion(f32[512]{0:T(512)S(1)} %copy-done.2, s32[1280]{0:T(1024)S(1)} %fusion.383, f32[1280]{0:T(1024)S(1)} %reshape.167), kind=kCustom, calls=%fused_computation.5 | custom fusion | flops 1280 | bytes 20480 | tf_op jit(solution)/shard_map/scatter-add | solution.py:97
  190.2 4.8 %collective-permute-start.32 = (f32[12,2,128]{2,0,1:T(8,128)S(1)}, f32[12,2,128]{2,0,1:T(8,128)S(1)}, u32[]{:S(2)}, u32[]{:S(2)}) collective-permute-start(f32[12,2,128]{2,0,1:T(8,128)S(1)} %get-tuple-element.26), channel_id=1, source_target_pairs={{0,4},{4,8},{8,12},{12,16},{16,20},{20,24},{24,28},{1,5},{5,9},{9,... | collective-permute-start | bytes 36872 | tf_op jit(solution)/shard_map/ppermute | solution.py:22
  205.7 4.1 %collective-permute-done.35 = f32[12,20,2]{2,0,1:T(8,128)S(1)} collective-permute-done((f32[12,20,2]{2,0,1:T(8,128)S(1)}, f32[12,20,2]{2,0,1:T(8,128)S(1)}, u32[]{:S(2)}, u32[]{:S(2)}) %collective-permute-start.35) | collective-permute-done | bytes 1952 | tf_op jit(solution)/shard_map/ppermute | solution.py:23
  210.2 5.5 %collective-permute-start.36 = (f32[2,16,128]{2,0,1:T(2,128)S(1)}, f32[2,16,128]{2,0,1:T(2,128)S(1)}, u32[]{:S(2)}, u32[]{:S(2)}) collective-permute-start(f32[2,16,128]{2,0,1:T(2,128)S(1)} %get-tuple-element.40), channel_id=1, source_target_pairs={{0,32},{32,64},{64,96},{96,128},{128,160},{160,192},{192,224},{224... | collective-permute-start | bytes 49160 | tf_op jit(solution)/shard_map/ppermute | solution.py:22
  217.1 8.0 %gather_fusion.1 = f32[1280]{0:T(1024)S(1)} fusion(f32[512]{0:T(512)S(1)} %bitcast.143, s32[2048]{0:T(1024)S(1)} %pad_clamp_fusion), kind=kCustom, calls=%fused_computation.1 | custom fusion | bytes 15360 | tf_op jit(solution)/shard_map/gather | solution.py:101
  225.8 6.8 %all-to-all-start.2 = ((f32[32,1,40]{2,1,0:T(1,128)}), f32[32,1,40]{2,1,0:T(1,128)S(1)}, u32[]{:S(2)}, u32[]{:S(2)}) async-start(f32[32,1,40]{2,1,0:T(1,128)} %all_to_all.22), calls=%async_computation.2 | async-start | bytes 32768 | tf_op jit(solution)/shard_map/all_to_all | solution.py:102
  252.9 4.3 %collective-permute-start.42 = (f32[2,16,128]{2,0,1:T(2,128)S(1)}, f32[2,16,128]{2,0,1:T(2,128)S(1)}, u32[]{:S(2)}, u32[]{:S(2)}) collective-permute-start(f32[2,16,128]{2,0,1:T(2,128)S(1)} %get-tuple-element.38), channel_id=1, source_target_pairs={{0,32},{32,64},{64,96},{96,128},{128,160},{160,192},{192,224},{224... | collective-permute-start | bytes 49160 | tf_op jit(solution)/shard_map/ppermute | solution.py:22
  258.8 11.3 %scatter_custom_fusion.3 = f32[16384]{0:T(1024)S(1)} fusion(s32[2048]{0:T(1024)S(1)} %bitcast.152, f32[2048]{0:T(1024)S(1)} %reshape.175, f32[]{:T(128)} %constant.55.clone.1), kind=kCustom, calls=%fused_computation.474 | custom fusion | flops 2048 | bytes 65540 | tf_op jit(solution)/shard_map/scatter-add | solution.py:109
  270.1 4.7 %collective-permute-start.44 = (f32[12,2,128]{2,0,1:T(8,128)S(1)}, f32[12,2,128]{2,0,1:T(8,128)S(1)}, u32[]{:S(2)}, u32[]{:S(2)}) collective-permute-start(f32[12,2,128]{2,0,1:T(8,128)S(1)} %get-tuple-element.22), channel_id=1, source_target_pairs={{0,4},{4,8},{8,12},{12,16},{16,20},{20,24},{24,28},{1,5},{5,9},{9,... | collective-permute-start | bytes 36872 | tf_op jit(solution)/shard_map/ppermute | solution.py:22
  285.6 4.1 %collective-permute-done.47 = f32[12,20,2]{2,0,1:T(8,128)S(1)} collective-permute-done((f32[12,20,2]{2,0,1:T(8,128)S(1)}, f32[12,20,2]{2,0,1:T(8,128)S(1)}, u32[]{:S(2)}, u32[]{:S(2)}) %collective-permute-start.47) | collective-permute-done | bytes 1952 | tf_op jit(solution)/shard_map/ppermute | solution.py:23
  (245 shorter events, 151.0 us)
Async XLA Ops:
  10.7 8.0 %collective-permute-start.2 = (f32[12,2,128]{2,0,1:T(8,128)S(1)}, f32[12,2,128]{2,0,1:T(8,128)S(1)}, u32[]{:S(2)}, u32[]{:S(2)}) collective-permute-start(f32[12,2,128]{2,0,1:T(8,128)S(1)} %get-tuple-element.36), channel_id=1, source_target_pairs={{0,4},{4,8},{8,12},{12,16},{16,20},{20,24},{24,28},{1,5},{5,9},{9,... | collective-permute-start | bytes 36872 | tf_op jit(solution)/shard_map/ppermute | solution.py:22
  40.7 7.9 %collective-permute-start.8 = (f32[12,2,128]{2,0,1:T(8,128)S(1)}, f32[12,2,128]{2,0,1:T(8,128)S(1)}, u32[]{:S(2)}, u32[]{:S(2)}) collective-permute-start(f32[12,2,128]{2,0,1:T(8,128)S(1)} %get-tuple-element.34), channel_id=1, source_target_pairs={{0,4},{4,8},{8,12},{12,16},{16,20},{20,24},{24,28},{1,5},{5,9},{9,... | collective-permute-start | bytes 36872 | tf_op jit(solution)/shard_map/ppermute | solution.py:22
  71.1 16.0 %collective-permute-start.14 = (f32[12,2,128]{2,0,1:T(8,128)S(1)}, f32[12,2,128]{2,0,1:T(8,128)S(1)}, u32[]{:S(2)}, u32[]{:S(2)}) collective-permute-start(f32[12,2,128]{2,0,1:T(8,128)S(1)} %get-tuple-element.32), channel_id=1, source_target_pairs={{0,4},{4,8},{8,12},{12,16},{16,20},{20,24},{24,28},{1,5},{5,9},{9,... | collective-permute-start | bytes 36872 | tf_op jit(solution)/shard_map/ppermute | solution.py:22
  76.0 11.1 %collective-permute-start.15 = (f32[12,2,128]{2,0,1:T(8,128)S(1)}, f32[12,2,128]{2,0,1:T(8,128)S(1)}, u32[]{:S(2)}, u32[]{:S(2)}) collective-permute-start(f32[12,2,128]{2,0,1:T(8,128)S(1)} %get-tuple-element.33), channel_id=1, source_target_pairs={{4,0},{8,4},{12,8},{16,12},{20,16},{24,20},{28,24},{5,1},{9,5},{13... | collective-permute-start | bytes 36872 | tf_op jit(solution)/shard_map/ppermute | solution.py:23
  81.3 74.3 %all-to-all-start = ((s32[32,1,40]{2,1,0:T(1,128)}), s32[32,1,40]{2,1,0:T(1,128)S(1)}, u32[]{:S(2)}, u32[]{:S(2)}) async-start(s32[32,1,40]{2,1,0:T(1,128)} %all_to_all.18), calls=%async_computation | async-start | bytes 32768 | tf_op jit(solution)/shard_map/all_to_all | solution.py:88
  90.6 7.0 %collective-permute-start.17 = (f32[12,20,2]{2,0,1:T(8,128)S(1)}, f32[12,20,2]{2,0,1:T(8,128)S(1)}, u32[]{:S(2)}, u32[]{:S(2)}) collective-permute-start(f32[12,20,2]{2,0,1:T(8,128)S(1)} %get-tuple-element.17), channel_id=1, source_target_pairs={{1,0},{2,1},{3,2},{5,4},{6,5},{7,6},{9,8},{10,9},{11,10},{13,12},{... | collective-permute-start | bytes 5768 | tf_op jit(solution)/shard_map/ppermute | solution.py:23
  106.3 8.0 %collective-permute-start.20 = (f32[12,2,128]{2,0,1:T(8,128)S(1)}, f32[12,2,128]{2,0,1:T(8,128)S(1)}, u32[]{:S(2)}, u32[]{:S(2)}) collective-permute-start(f32[12,2,128]{2,0,1:T(8,128)S(1)} %get-tuple-element.30), channel_id=1, source_target_pairs={{0,4},{4,8},{8,12},{12,16},{16,20},{20,24},{24,28},{1,5},{5,9},{9,... | collective-permute-start | bytes 36872 | tf_op jit(solution)/shard_map/ppermute | solution.py:22
  127.4 18.4 %collective-permute-start.24 = (f32[2,16,128]{2,0,1:T(2,128)S(1)}, f32[2,16,128]{2,0,1:T(2,128)S(1)}, u32[]{:S(2)}, u32[]{:S(2)}) collective-permute-start(f32[2,16,128]{2,0,1:T(2,128)S(1)} %get-tuple-element.44), channel_id=1, source_target_pairs={{0,32},{32,64},{64,96},{96,128},{128,160},{160,192},{192,224},{224... | collective-permute-start | bytes 49160 | tf_op jit(solution)/shard_map/ppermute | solution.py:22
  131.8 14.0 %collective-permute-start.25 = (f32[2,16,128]{2,0,1:T(2,128)S(1)}, f32[2,16,128]{2,0,1:T(2,128)S(1)}, u32[]{:S(2)}, u32[]{:S(2)}) collective-permute-start(f32[2,16,128]{2,0,1:T(2,128)S(1)} %get-tuple-element.45), channel_id=1, source_target_pairs={{32,0},{64,32},{96,64},{128,96},{160,128},{192,160},{224,192},{256... | collective-permute-start | bytes 49160 | tf_op jit(solution)/shard_map/ppermute | solution.py:23
  145.8 17.0 %collective-permute-start.26 = (f32[12,2,128]{2,0,1:T(8,128)S(1)}, f32[12,2,128]{2,0,1:T(8,128)S(1)}, u32[]{:S(2)}, u32[]{:S(2)}) collective-permute-start(f32[12,2,128]{2,0,1:T(8,128)S(1)} %get-tuple-element.28), channel_id=1, source_target_pairs={{0,4},{4,8},{8,12},{12,16},{16,20},{20,24},{24,28},{1,5},{5,9},{9,... | collective-permute-start | bytes 36872 | tf_op jit(solution)/shard_map/ppermute | solution.py:22
  150.4 12.5 %collective-permute-start.27 = (f32[12,2,128]{2,0,1:T(8,128)S(1)}, f32[12,2,128]{2,0,1:T(8,128)S(1)}, u32[]{:S(2)}, u32[]{:S(2)}) collective-permute-start(f32[12,2,128]{2,0,1:T(8,128)S(1)} %get-tuple-element.29), channel_id=1, source_target_pairs={{4,0},{8,4},{12,8},{16,12},{20,16},{24,20},{28,24},{5,1},{9,5},{13... | collective-permute-start | bytes 36872 | tf_op jit(solution)/shard_map/ppermute | solution.py:23
  155.6 23.7 %all-to-all-start.1 = ((f32[32,1,40]{2,1,0:T(1,128)}), f32[32,1,40]{2,1,0:T(1,128)S(1)}, u32[]{:S(2)}, u32[]{:S(2)}) async-start(f32[32,1,40]{2,1,0:T(1,128)} %all_to_all.20), calls=%async_computation.1 | async-start | bytes 32768 | tf_op jit(solution)/shard_map/all_to_all | solution.py:81
  166.3 7.0 %collective-permute-start.29 = (f32[12,20,2]{2,0,1:T(8,128)S(1)}, f32[12,20,2]{2,0,1:T(8,128)S(1)}, u32[]{:S(2)}, u32[]{:S(2)}) collective-permute-start(f32[12,20,2]{2,0,1:T(8,128)S(1)} %get-tuple-element.13), channel_id=1, source_target_pairs={{1,0},{2,1},{3,2},{5,4},{6,5},{7,6},{9,8},{10,9},{11,10},{13,12},{... | collective-permute-start | bytes 5768 | tf_op jit(solution)/shard_map/ppermute | solution.py:23
  173.7 16.4 %collective-permute-start.30 = (f32[2,16,128]{2,0,1:T(2,128)S(1)}, f32[2,16,128]{2,0,1:T(2,128)S(1)}, u32[]{:S(2)}, u32[]{:S(2)}) collective-permute-start(f32[2,16,128]{2,0,1:T(2,128)S(1)} %get-tuple-element.42), channel_id=1, source_target_pairs={{0,32},{32,64},{64,96},{96,128},{128,160},{160,192},{192,224},{224... | collective-permute-start | bytes 49160 | tf_op jit(solution)/shard_map/ppermute | solution.py:22
  178.0 12.1 %collective-permute-start.31 = (f32[2,16,128]{2,0,1:T(2,128)S(1)}, f32[2,16,128]{2,0,1:T(2,128)S(1)}, u32[]{:S(2)}, u32[]{:S(2)}) collective-permute-start(f32[2,16,128]{2,0,1:T(2,128)S(1)} %get-tuple-element.43), channel_id=1, source_target_pairs={{32,0},{64,32},{96,64},{128,96},{160,128},{192,160},{224,192},{256... | collective-permute-start | bytes 49160 | tf_op jit(solution)/shard_map/ppermute | solution.py:23
  190.2 7.5 %collective-permute-start.32 = (f32[12,2,128]{2,0,1:T(8,128)S(1)}, f32[12,2,128]{2,0,1:T(8,128)S(1)}, u32[]{:S(2)}, u32[]{:S(2)}) collective-permute-start(f32[12,2,128]{2,0,1:T(8,128)S(1)} %get-tuple-element.26), channel_id=1, source_target_pairs={{0,4},{4,8},{8,12},{12,16},{16,20},{20,24},{24,28},{1,5},{5,9},{9,... | collective-permute-start | bytes 36872 | tf_op jit(solution)/shard_map/ppermute | solution.py:22
  210.2 22.4 %collective-permute-start.36 = (f32[2,16,128]{2,0,1:T(2,128)S(1)}, f32[2,16,128]{2,0,1:T(2,128)S(1)}, u32[]{:S(2)}, u32[]{:S(2)}) collective-permute-start(f32[2,16,128]{2,0,1:T(2,128)S(1)} %get-tuple-element.40), channel_id=1, source_target_pairs={{0,32},{32,64},{64,96},{96,128},{128,160},{160,192},{192,224},{224... | collective-permute-start | bytes 49160 | tf_op jit(solution)/shard_map/ppermute | solution.py:22
  215.7 16.9 %collective-permute-start.37 = (f32[2,16,128]{2,0,1:T(2,128)S(1)}, f32[2,16,128]{2,0,1:T(2,128)S(1)}, u32[]{:S(2)}, u32[]{:S(2)}) collective-permute-start(f32[2,16,128]{2,0,1:T(2,128)S(1)} %get-tuple-element.41), channel_id=1, source_target_pairs={{32,0},{64,32},{96,64},{128,96},{160,128},{192,160},{224,192},{256... | collective-permute-start | bytes 49160 | tf_op jit(solution)/shard_map/ppermute | solution.py:23
  225.8 13.7 %all-to-all-start.2 = ((f32[32,1,40]{2,1,0:T(1,128)}), f32[32,1,40]{2,1,0:T(1,128)S(1)}, u32[]{:S(2)}, u32[]{:S(2)}) async-start(f32[32,1,40]{2,1,0:T(1,128)} %all_to_all.22), calls=%async_computation.2 | async-start | bytes 32768 | tf_op jit(solution)/shard_map/all_to_all | solution.py:102
  232.6 10.8 %collective-permute-start.38 = (f32[12,2,128]{2,0,1:T(8,128)S(1)}, f32[12,2,128]{2,0,1:T(8,128)S(1)}, u32[]{:S(2)}, u32[]{:S(2)}) collective-permute-start(f32[12,2,128]{2,0,1:T(8,128)S(1)} %get-tuple-element.24), channel_id=1, source_target_pairs={{0,4},{4,8},{8,12},{12,16},{16,20},{20,24},{24,28},{1,5},{5,9},{9,... | collective-permute-start | bytes 36872 | tf_op jit(solution)/shard_map/ppermute | solution.py:22
  236.2 7.2 %collective-permute-start.39 = (f32[12,2,128]{2,0,1:T(8,128)S(1)}, f32[12,2,128]{2,0,1:T(8,128)S(1)}, u32[]{:S(2)}, u32[]{:S(2)}) collective-permute-start(f32[12,2,128]{2,0,1:T(8,128)S(1)} %get-tuple-element.25), channel_id=1, source_target_pairs={{4,0},{8,4},{12,8},{16,12},{20,16},{24,20},{28,24},{5,1},{9,5},{13... | collective-permute-start | bytes 36872 | tf_op jit(solution)/shard_map/ppermute | solution.py:23
  245.8 6.7 %collective-permute-start.41 = (f32[12,20,2]{2,0,1:T(8,128)S(1)}, f32[12,20,2]{2,0,1:T(8,128)S(1)}, u32[]{:S(2)}, u32[]{:S(2)}) collective-permute-start(f32[12,20,2]{2,0,1:T(8,128)S(1)} %get-tuple-element.9), channel_id=1, source_target_pairs={{1,0},{2,1},{3,2},{5,4},{6,5},{7,6},{9,8},{10,9},{11,10},{13,12},{... | collective-permute-start | bytes 5768 | tf_op jit(solution)/shard_map/ppermute | solution.py:23
  252.9 17.2 %collective-permute-start.42 = (f32[2,16,128]{2,0,1:T(2,128)S(1)}, f32[2,16,128]{2,0,1:T(2,128)S(1)}, u32[]{:S(2)}, u32[]{:S(2)}) collective-permute-start(f32[2,16,128]{2,0,1:T(2,128)S(1)} %get-tuple-element.38), channel_id=1, source_target_pairs={{0,32},{32,64},{64,96},{96,128},{128,160},{160,192},{192,224},{224... | collective-permute-start | bytes 49160 | tf_op jit(solution)/shard_map/ppermute | solution.py:22
  257.1 12.9 %collective-permute-start.43 = (f32[2,16,128]{2,0,1:T(2,128)S(1)}, f32[2,16,128]{2,0,1:T(2,128)S(1)}, u32[]{:S(2)}, u32[]{:S(2)}) collective-permute-start(f32[2,16,128]{2,0,1:T(2,128)S(1)} %get-tuple-element.39), channel_id=1, source_target_pairs={{32,0},{64,32},{96,64},{128,96},{160,128},{192,160},{224,192},{256... | collective-permute-start | bytes 49160 | tf_op jit(solution)/shard_map/ppermute | solution.py:23
  (40 other events, 431.4 us)
where the time goes:
time: 296 us; the launch traced here: 291 us
  starting transfers between devices  153 us (52%)
  waiting for transfers between devices  65.1 us (22%)
  local copies, waits for them, and re-layouts  37.9 us (13%)
  other arithmetic  24.8 us (8%)
  matrix products  7.46 us (3%)
    ppermute x24, starting transfers between devices, padded_2(): before = lax.ppermute(last, axis, up)  97.6 us
    ppermute x24, waiting for transfers between devices, padded_2(): after = lax.ppermute(initial, axis, down)  57.6 us
    ppermute x24, starting transfers between devices, padded_2(): after = lax.ppermute(initial, axis, down)  37.3 us
    gather x2, local copies, waits for them, and re-layouts, shards(): flux = jnp.sum(face_weight * flat_cells[face_cells], axis=1)  12 us
    scatter-add x1, other arithmetic, shards(): coupled = jnp.zeros(flat_cells.shape, jnp.float32).at[face_cells.reshape(...  11.3 us
    scatter-add x1, other arithmetic, shards(): jnp.zeros(solid_source.shape, jnp.float32).at[arrived_cells]  9.38 us
    gather x1, local copies, waits for them, and re-layouts, shards(): returned = solid_result[arrived_cells]  7.99 us
    dot_general x24, matrix products, block_apply(): jnp.einsum(FORMS[along], operand, matrix, precision=lax.Precision.HIGHEST)  6.86 us
  transfers between devices with their start and end apart: 51, of which 25 were waited for; matrix products, arithmetic and copies ran while one was open for 21% of the time, Pallas kernels for 0%

commit v1 on v0

v1 whole, which is shorter than its diff:
```python
import math
import jax
import jax.numpy as jnp
from jax import lax
from jax.experimental import pallas as pl
from jax.experimental.pallas import tpu as pltpu
from jax.sharding import PartitionSpec as P

SWEEPS = 8
RELAX = 0.15
SPREAD = 0.06
COUPLE = 0.5
SHIFT = 0.25

F32 = jnp.float32
BF16 = jnp.bfloat16
VMEM_LIMIT = 16 * 1024 * 1024
HI = lax.Precision.HIGHEST


def iota(shape, dim):
    return lax.broadcasted_iota(jnp.int32, shape, dim)


def dot(a, b, dims=((1,), (0,)), precision=HI):
    return lax.dot_general(a, b, (dims, ((), ())), precision=precision, preferred_element_type=F32)


def narrow_dot(a, b, dims=((1,), (0,))):
    return lax.dot_general(a, b, (dims, ((), ())), preferred_element_type=F32)


def split2(v):
    p1 = v.astype(BF16)
    return p1, (v - p1.astype(F32)).astype(BF16)


def split3(v):
    p1 = v.astype(BF16)
    rest = v - p1.astype(F32)
    p2 = rest.astype(BF16)
    p3 = (rest - p2.astype(F32)).astype(BF16)
    return p1, p2, p3


def hot_dot(values, hot, dims):
    parts = [narrow_dot(p, hot, dims) for p in split3(values)]
    return parts[0] + (parts[1] + parts[2])


def hot_rows(index_row, count):
    return iota((count, index_row.shape[1]), 0) == index_row


def ones_of(mask):
    return jnp.where(mask, 1.0, 0.0).astype(BF16)


def weights_of(far):
    return jnp.where(
        far == 0, -30.0 / 12.0, jnp.where(far == 1, 16.0 / 12.0, jnp.where(far == 2, -1.0 / 12.0, 0.0))
    )


VM = pl.BlockSpec(memory_space=pltpu.VMEM)
ANY = pl.BlockSpec(memory_space=pl.ANY)


def call(body, outs, *args, specs=None, scratch=(), limit=VMEM_LIMIT, flops=1000000, touched=100000):
    return pl.pallas_call(
        body,
        out_shape=outs,
        in_specs=[VM] * len(args) if specs is None else specs,
        out_specs=jax.tree.map(lambda _: VM, outs),
        scratch_shapes=list(scratch),
        compiler_params=pltpu.CompilerParams(vmem_limit_bytes=limit),
        cost_estimate=pl.CostEstimate(flops=flops, bytes_accessed=touched, transcendentals=0),
    )(*args)


def load_all(sem, pairs):
    copies = [pltpu.make_async_copy(src, dst, sem.at[n]) for n, (src, dst) in enumerate(pairs)]
    for c in copies:
        c.start()
    for c in copies:
        c.wait()


def wide_dot(a, b):
    high, low = split2(b)
    return narrow_dot(a[0], high) + (narrow_dot(a[0], low) + narrow_dot(a[1], high))


def put_split(ref, cols, value):
    high, low = split2(value)
    ref[0, :, cols] = high
    ref[1, :, cols] = low


def pack_body(table_hbm, source_hbm, inv_hbm, out_ref, table_ref, source_ref, inv_ref, sem):
    load_all(sem, [(table_hbm, table_ref), (source_hbm, source_ref), (inv_hbm, inv_ref)])
    inv = jnp.concatenate([inv_ref[r : r + 1, :] for r in range(8)] + [jnp.zeros((1, 64), F32)], axis=1)
    for y in range(16):
        out_ref[17 * y : 17 * y + 8, :] = table_ref[pl.ds(y, 8, stride=16), :]
        out_ref[17 * y + 8 : 17 * y + 16, :] = source_ref[pl.ds(y, 8, stride=16), :]
        out_ref[17 * y + 16 : 17 * y + 17, :] = inv


def lines_body(recv_ref, out_ref, token_ref, power):
    token_ref[...] = jnp.zeros((8, 128), F32)
    row, col = iota((128, 128), 0), iota((128, 128), 1)
    inv = recv_ref[pl.ds(16, 16, stride=17), :]
    rows = jnp.where((iota((128, 16), 0) >> 3) == iota((128, 16), 1), 1.0, 0.0).astype(BF16)
    first, second = split2(inv)
    wide = narrow_dot(rows, first) + narrow_dot(rows, second)
    wide = jnp.where((row & 7) == (col & 7), wide, 0.0)
    pick = ones_of((row < 64) & ((row >> 3) == (col & 7)))
    first, second = split2(wide)
    diag = narrow_dot(first, pick) + narrow_dot(second, pick)
    diag = jnp.where((row >> 3) == (col >> 3), diag, 0.0)
    far = jnp.abs(row - col)
    first, second = split2(diag)
    band = jnp.where(far == 0, -30.0, jnp.where(far == 1, 16.0, jnp.where(far == 2, -1.0, 0.0))).astype(BF16)
    op = (SPREAD / 12.0) * (narrow_dot(first, band) + narrow_dot(second, band)) + jnp.where(far == 0, SHIFT, 0.0)
    for f in range(2):
        power[:, 128 * f : 128 * f + 128] = jnp.concatenate(
            [recv_ref[17 * g + 8 * f : 17 * g + 8 * f + 8, :] for g in range(16)], axis=0
        )

    def store(k, value):
        power[:, 256 * k : 256 * k + value.shape[1]] = value

    both = wide_dot(split2(op), jnp.concatenate([op, power[:, 0:256]], axis=1))
    store(1, both[:, 128:])
    both = wide_dot(split2(both[:, 0:128]), jnp.concatenate([both[:, 0:128], power[:, 0:512]], axis=1))
    store(2, both[:, 128:])
    four = split2(both[:, 0:128])
    store(4, wide_dot(four, power[:, 0:1024]))
    store(8, wide_dot(four, power[:, 1024 : 1024 + 128]))
    for m in range(SWEEPS - 1):
        total = float(math.comb(SWEEPS, m)) * power[:, 256 * (SWEEPS - m) : 256 * (SWEEPS - m) + 128]
        for i in range(m, SWEEPS):
            total = total + RELAX * math.comb(i, m) * power[:, 256 * (i - m) + 128 : 256 * (i - m) + 256]
        for g in range(16):
            out_ref[56 * g + 8 * m : 56 * g + 8 * m + 8, :] = total[8 * g : 8 * g + 8]


def near_body(table_ref, low_ref, high_ref, source_hbm, inv_ref, out_ref, source_ref, sem):
    load_all(sem, [(source_hbm, source_ref)])
    layers = [low_ref[0:16, :], low_ref[16:32, :]]
    layers += [table_ref[16 * x : 16 * x + 16, :] for x in range(8)]
    layers += [high_ref[0:16, :], high_ref[16:32, :]]
    sums = [
        16.0 * (layers[x + 1] + layers[x + 3]) - 30.0 * layers[x + 2] - layers[x] - layers[x + 4] for x in range(8)
    ]
    for i in range(8):
        total = sums[0] * inv_ref[0, i]
        for r in range(1, 8):
            total = total + sums[r] * inv_ref[r, i]
        total = (SPREAD / 12.0) * total + SHIFT * layers[i + 2]
        rows = slice(16 * i, 16 * i + 16)
        out_ref[rows, :] = SWEEPS * total + RELAX * source_ref[rows, :]


def deal_body(recv_ref, table_ref, near_ref, heat_ref, rows_ref, after_one, after_two, out_ref, first_ref):
    for m in range(SWEEPS - 1):
        for y in range(16):
            rows = recv_ref[56 * y + 8 * m : 56 * y + 8 * m + 8, :]
            if m == 0:
                first_ref[pl.ds(y, 8, stride=16), :] = rows
            else:
                q, half = divmod(m - 1, 2)
                out_ref[pl.ds(40 * q + 16 * half + y, 8, stride=160), :] = rows
    for x in range(8):
        out_ref[160 * x + 120 : 160 * x + 136, :] = near_ref[16 * x : 16 * x + 16, :]
        out_ref[160 * x + 136 : 160 * x + 152, :] = table_ref[16 * x : 16 * x + 16, :]
    for h in range(4):
        out_ref[pl.ds(32 + h, 32, stride=40), :] = heat_ref[h * 32 : (h + 1) * 32, :]
    for o in range(32):
        out_ref[40 * o + 36 : 40 * o + 40, :] = rows_ref[0:4, :]


def send_body(table_ref, cells_ref, weight_ref, owner_ref, solid_ref, inv_y_ref, inv_z_in, after_ref, out_ref, rows_ref, inv_z_ref, low_ref, high_ref):
    gy = lax.axis_index("gy")
    gz = lax.axis_index("gz")
    inv_z_ref[...] = inv_z_in[...]
    low_ref[...] = table_ref[0:32, :]
    high_ref[...] = table_ref[96:128, :]
    table = table_ref[...]
    acc = None
    for k in range(4):
        cell = cells_ref[k : k + 1, :]
        hot = ones_of(hot_rows(cell >> 7, 128))
        spread = jnp.where(hot_rows(cell & 127, 128), weight_ref[k : k + 1, :], 0.0)
        term = hot_dot(table, hot, ((0,), (0,))) * spread
        acc = term if acc is None else acc + term
    flux = jnp.sum(acc, axis=0, keepdims=True)
    solid = solid_ref[...]
    owner = owner_ref[...]
    rank = (owner & 3) * 8 + (owner >> 2)
    hot_hi = ones_of(hot_rows((solid >> 7) * 32 + rank, 128))
    out_ref[...] = hot_dot(jnp.where(hot_rows(solid & 127, 128), flux, 0.0), hot_hi, ((1,), (1,))).T
    shift = iota((16, 128), 1) - gy * 16 - iota((16, 128), 0)
    own = SPREAD * dot(inv_y_ref[...], weights_of(jnp.abs(shift)), ((0,), (0,)))
    own = own + jnp.where(shift == 0, 1.0 - RELAX - SHIFT, 0.0)
    pick = jnp.where(iota((8, 16), 1) == iota((8, 16), 0) + gz * 4, 1.0, 0.0)
    rows_ref[...] = dot(pick, own)


def split_body(value_hbm, after_hbm, out_ref, value_ref, sem):
    load_all(sem, [(value_hbm, value_ref)])
    put_split(out_ref, slice(0, 512), value_ref[...])


def finish_body(recv_ref, first_ref, cells_ref, weight_ref, owner_ref, solid_ref, out_ref, stage):
    for o in range(32):
        owner = (o % 8) * 4 + o // 8
        stage[4 * owner : 4 * owner + 4, :] = recv_ref[20 * o + 16 : 20 * o + 20, :]
    solid = solid_ref[...]
    hot = ones_of(hot_rows(owner_ref[...] * 4 + (solid >> 7), 128))
    high, rest = split2(stage[...])
    picked = narrow_dot(high, hot, ((0,), (0,))) + narrow_dot(rest, hot, ((0,), (0,)))
    temp = COUPLE * jnp.sum(jnp.where(hot_rows(solid & 127, 128), picked, 0.0), axis=0, keepdims=True)
    hots, highs, rests = [], [], []
    for k in range(4):
        cell = cells_ref[k : k + 1, :]
        hots.append(ones_of(hot_rows(cell >> 7, 128)))
        high, rest = split2(jnp.where(hot_rows(cell & 127, 128), temp * weight_ref[k : k + 1, :], 0.0))
        highs.append(high)
        rests.append(rest)
    hot = jnp.concatenate(hots, axis=1)
    total = narrow_dot(hot, jnp.concatenate(highs, axis=1), ((1,), (1,)))
    total = total + narrow_dot(hot, jnp.concatenate(rests, axis=1), ((1,), (1,)))
    for i in range(8):
        parts = [recv_ref[20 * o : 20 * o + 16, :] for o in range(4 * i, 4 * i + 4)]
        part = (parts[0] + parts[1]) + (parts[2] + parts[3])
        rows = slice(16 * i, 16 * i + 16)
        out_ref[i] = part + first_ref[rows, :] + total[rows, :]


def prepare_body(own_ref, one_ref, two_ref, three_ref, op_z_ref, mats):
    gz = lax.axis_index("gz")
    for d, ref in enumerate((own_ref, one_ref, two_ref, three_ref)):
        mats[jnp.bitwise_xor(gz, d)] = ref[...]
    for k in range(4):
        far = jnp.abs(iota((512, 128), 0) - (iota((512, 128), 1) + 128 * k))
        put_split(op_z_ref, slice(128 * k, 128 * k + 128), SPREAD * dot(weights_of(far), mats[k]))


def planes_body(recv_ref, op_z_ref, source_ref, inverse_ref, out_ref, line_ref, low, acc, op_y):
    q = lax.rem(lax.axis_index("gy"), 4)
    for o in range(32):
        z, y = divmod(o, 8)
        low[16 * y : 16 * y + 16, 128 * z : 128 * (z + 1)] = recv_ref[o, 0:16]
        acc[16 * y : 16 * y + 16, 128 * z : 128 * (z + 1)] = recv_ref[o, 16:32]
        op_y[16 * y + 4 * z : 16 * y + 4 * z + 4, :] = recv_ref[o, 36:40]
    y_high, y_low = split2(op_y[...])
    y_both = jnp.concatenate([y_high, y_high], axis=1)

    def apply():
        high, rest = split2(acc[...])
        along_y = narrow_dot(y_both, jnp.concatenate([high, rest], axis=0)) + narrow_dot(y_low, high)
        along_z = narrow_dot(high, op_z_ref[0]) + (narrow_dot(high, op_z_ref[1]) + narrow_dot(rest, op_z_ref[0]))
        return along_y + along_z

    heat = jnp.sum(recv_ref[:, 32:40, :], axis=0)[0:4, :] + source_ref[...]
    high, rest = split2(jnp.concatenate([heat[h : h + 1, :] for h in range(4)], axis=1))
    both = jnp.concatenate([high.astype(F32), rest.astype(F32), jnp.zeros((6, 512), F32)], axis=0).astype(BF16)
    result = narrow_dot(both, inverse_ref[0])
    result = (result[0:1] + result[1:2]) + narrow_dot(both, inverse_ref[1])[0:1]
    line_ref[...] = result
    rows = jnp.concatenate([result[:, 128 * h : 128 * (h + 1)] for h in range(4)], axis=0)
    for o in range(32):
        out_ref[20 * o + 16 : 20 * o + 20, :] = rows

    acc[...] = apply() + low[...]

    def step(_, c):
        acc[...] = apply()
        return c

    lax.fori_loop(0, 2 * q + 1, step, 0)
    for o in range(32):
        z, y = divmod(o, 8)
        out_ref[20 * o : 20 * o + 16, :] = acc[16 * y : 16 * y + 16, 128 * z : 128 * (z + 1)]


def exchange(v, axes):
    return lax.all_to_all(v, axes, split_axis=0, concat_axis=0, tiled=True)


def shards(
    fluid_adjoint,
    fluid_source,
    inverse_x,
    inverse_y,
    inverse_z,
    face_cells,
    face_weight,
    face_owner,
    face_solid,
    solid_inverse,
    solid_source,
):
    shape = jax.ShapeDtypeStruct
    group = ("gz", "gy")
    block = shape((128, 128), F32)
    block_vmem = pltpu.VMEM((128, 128), F32)
    dma = pltpu.SemaphoreType.DMA
    packed, table = call(
        pack_body,
        (shape((16 * 17, 128), F32), block),
        fluid_adjoint.reshape(128, 128),
        fluid_source.reshape(128, 128),
        inverse_x,
        specs=[ANY] * 3,
        scratch=[block_vmem, pltpu.VMEM((8, 8), F32), dma((3,))],
        limit=None,
    )
    lines = exchange(packed.reshape(16, 17, 1, 128), "gx").reshape(16 * 17, 128)

    face_args = (face_cells.T, face_weight.T, face_owner.reshape(1, 512), face_solid.reshape(1, 512))
    terms, token = call(
        lines_body,
        (shape((896, 128), F32), shape((8, 128), F32)),
        lines,
        scratch=[pltpu.VMEM((128, 256 * (SWEEPS + 1)), F32)],
    )
    back = exchange(terms.reshape(16, 56, 128), "gx").reshape(896, 128)

    heat, y_rows, inv_z, low, high = call(
        send_body,
        (block, shape((8, 128), F32), block, shape((32, 128), F32), shape((32, 128), F32)),
        table,
        *face_args,
        inverse_y,
        inverse_z,
        token,
    )
    others = [lax.ppermute(inv_z, "gz", [(i, i ^ d) for i in range(4)]) for d in (1, 2, 3)]
    op_z = call(
        prepare_body,
        shape((2, 512, 512), BF16),
        inv_z,
        *others,
        scratch=[pltpu.VMEM((4, 128, 128), F32)],
    )
    inverse = call(
        split_body,
        shape((2, 512, 512), BF16),
        solid_inverse,
        token,
        specs=[ANY] * 2,
        scratch=[pltpu.VMEM((512, 512), F32), dma((1,))],
    )

    up = [(i, i + 1) for i in range(15)]
    near = call(
        near_body,
        block,
        table,
        lax.ppermute(high, "gx", up),
        lax.ppermute(low, "gx", [(j, i) for i, j in up]),
        fluid_source.reshape(128, 128),
        inverse_x,
        specs=[VM] * 3 + [ANY, pl.BlockSpec(memory_space=pltpu.SMEM)],
        scratch=[block_vmem, dma((1,))],
    )

    dealt, first = call(
        deal_body,
        (shape((1280, 128), F32), block),
        back,
        table,
        near,
        heat,
        y_rows,
        op_z,
        inverse,
        specs=[VM] * 5 + [ANY] * 2,
    )
    planes = exchange(dealt.reshape(32, 40, 128), group)
    swept, solid_line = call(
        planes_body,
        (shape((640, 128), F32), shape((1, 512), F32)),
        planes,
        op_z,
        solid_source.reshape(4, 128),
        inverse,
        scratch=[pltpu.VMEM((128, 512), F32), pltpu.VMEM((128, 512), F32), block_vmem],
    )
    parts = exchange(swept.reshape(32, 20, 1, 128), group).reshape(640, 128)
    result = call(finish_body, shape((8, 16, 128), F32), parts, first, *face_args, scratch=[block_vmem])
    return result, solid_line.reshape(512)


def solution(mesh):
    in_specs = (
        P("gx", "gy", "gz"),
        P("gx", "gy", "gz"),
        P("gx", None),
        P("gy", None),
        P("gz", None),
        P(("gx", "gy", "gz"), None),
        P(("gx", "gy", "gz"), None),
        P(("gx", "gy", "gz"), None),
        P(("gx", "gy", "gz")),
        P(("gx", "gy", "gz"), None),
        P(("gx", "gy", "gz")),
    )
    out_specs = (P("gx", "gy", "gz"), P(("gx", "gy", "gz")))
    return jax.shard_map(shards, mesh=mesh, in_specs=in_specs, out_specs=out_specs, check_vma=False)
```

time: 296 us -> 107 us (0.36); the launches traced: 291 us -> 106 us
  starting transfers between devices: 153 us -> 20.4 us
  blocking collectives: 0 us -> 67.6 us
  waiting for transfers between devices: 65.1 us -> 5.02 us
  local copies, waits for them, and re-layouts: 37.9 us -> 0.68 us
  other arithmetic: 24.8 us -> 0 us
  Pallas kernels: 0 us -> 11.4 us
  matrix products: 7.46 us -> 0 us
    ppermute x48 -> x5, starting transfers between devices: 135 us -> 13.7 us  [the longest x3 9.05 us: shards(): lax.ppermute(inv_z, 'gz', [(i, i ^ d) for i in range(4)])]
    all_to_all x0 -> x3, blocking collectives: none -> 67.6 us  [exchange(): return lax.all_to_all(v, axes, split_axis=0, concat_axis=0, tiled=True)]
    ppermute x48 -> x5, waiting for transfers between devices: 63.8 us -> 5.02 us  [the longest x1 5.01 us: shards(): lax.ppermute(low, 'gx', [(j, i) for i, j in up])]
    gather x4 -> x0, local copies, waits for them, and re-layouts: 23.2 us -> none  [the longest x2 12 us: shards(): flux = jnp.sum(face_weight * flat_cells[face_cells], axis=1)]
    scatter-add x2 -> x0, other arithmetic: 20.7 us -> none  [the longest x1 11.3 us: shards(): coupled = jnp.zeros(flat_cells.shape, jnp.float32).at[face_cells.reshape(...]
    all_to_all x3 -> x1, starting transfers between devices: 18.2 us -> 6.72 us  [exchange(): return lax.all_to_all(v, axes, split_axis=0, concat_axis=0, tiled=True)]
    pallas_call x0 -> x9, Pallas kernels: none -> 11.4 us  [call(): pl.pallas_call(body, out_shape=outs, in_specs=[VM] * len(args) if specs i...]
    dot_general x25 -> x0, matrix products: 7.46 us -> none  [the longest x24 6.86 us: block_apply(): jnp.einsum(FORMS[along], operand, matrix, precision=lax.Precision.HIGHEST)]
  transfers between devices with their start and end apart: 51 -> 6, of which waited for: 25 -> 1; matrix products, arithmetic and copies ran while one was open for 21% -> 0% of each run, Pallas kernels for 0% -> 3%
where the time goes in v1:
time: 107 us; the launch traced here: 106 us
  blocking collectives  67.6 us (63%)
  starting transfers between devices  20.4 us (19%)
  Pallas kernels  11.4 us (11%)
  waiting for transfers between devices  5.02 us (5%)
    all_to_all x3, blocking collectives, exchange(): return lax.all_to_all(v, axes, split_axis=0, concat_axis=0, tiled=True)  67.6 us
    pallas_call x9, Pallas kernels, call(): pl.pallas_call(body, out_shape=outs, in_specs=[VM] * len(args) if specs i...  11.4 us
    ppermute x3, starting transfers between devices, shards(): lax.ppermute(inv_z, 'gz', [(i, i ^ d) for i in range(4)])  9.05 us
    all_to_all x1, starting transfers between devices, exchange(): return lax.all_to_all(v, axes, split_axis=0, concat_axis=0, tiled=True)  6.72 us
    ppermute x1, waiting for transfers between devices, shards(): lax.ppermute(low, 'gx', [(j, i) for i, j in up])  5.01 us
    ppermute x1, starting transfers between devices, shards(): lax.ppermute(high, 'gx', up)  3.25 us
  transfers between devices with their start and end apart: 6, of which 1 were waited for; matrix products, arithmetic and copies ran while one was open for 0% of the time, Pallas kernels for 3%

profile of v1, /device:TPU:1, one launch (start us, length us, event | category | flops | bytes accessed | tf_op | source)
XLA Modules:
  0.0 106.0 jit_solution(1456895967898703612)
XLA Ops:
  0.6 1.7 %shard_map.122 = (f32[272,128]{1,0:T(8,128)}, f32[128,128]{1,0:T(8,128)}) custom-call(f32[128,128]{1,0:T(8,128)} %bitcast.32, f32[128,128]{1,0:T(8,128)} %bitcast.20, f32[8,8]{1,0:T(8,128)} %inv_ref.1), custom_call_target="tpu_custom_call" | custom-call | flops 1000000 | bytes 100000 | tf_op jit(solution)/shard_map/pallas_call | solution.py:70
  2.4 27.8 %all_to_all.20 = f32[16,17,1,128]{3,2,1,0:T(1,128)S(1)} all-to-all(f32[16,17,1,128]{3,2,1,0:T(1,128)} %bitcast.31), channel_id=1, replica_groups=mesh['gx'=16,'gy'=8,'gz'=4] {'gx'}, dimensions={0} | all-to-all | bytes 278528 | tf_op jit(solution)/shard_map/all_to_all | solution.py:289
  30.2 2.2 %shard_map.123 = (f32[896,128]{1,0:T(8,128)}, f32[8,128]{1,0:T(8,128)S(1)}) custom-call(f32[272,128]{1,0:T(8,128)S(1)} %bitcast.18), custom_call_target="tpu_custom_call" | custom-call | flops 1000000 | bytes 100000 | tf_op jit(solution)/shard_map/pallas_call | solution.py:70
  32.4 0.0 copy-start.9
  32.4 6.7 %all-to-all-start.1 = ((f32[16,56,128]{2,1,0:T(8,128)}), f32[16,56,128]{2,1,0:T(8,128)S(1)}, u32[]{:S(2)}, u32[]{:S(2)}) async-start(f32[16,56,128]{2,1,0:T(8,128)} %bitcast.4), calls=%async_computation.1 | async-start | bytes 917504 | tf_op jit(solution)/shard_map/all_to_all | solution.py:289
  39.1 0.0 copy-start.4
  39.1 0.0 copy-start.7
  39.2 0.6 copy-done.4
  39.8 1.1 %shard_map.124 = (f32[128,128]{1,0:T(8,128)S(1)}, f32[8,128]{1,0:T(8,128)S(1)}, f32[128,128]{1,0:T(8,128)S(1)}, f32[32,128]{1,0:T(8,128)S(1)}, f32[32,128]{1,0:T(8,128)S(1)}) custom-call(f32[128,128]{1,0:T(8,128)S(1)} %copy-done.1, s32[4,512]{1,0:T(4,128)S(1)} %bitcast.22, f32[4,512]{1,0:T(4,128)S(1)} %bitcast.24, s32[1,512]{1,0:T(1,128)S(1)} %bitcast.26, ...), custom_call_target="tpu_custom_call" | custom-call | flops 1000000 | bytes 100000 | tf_op jit(solution)/shard_map/pallas_call | solution.py:70
  40.9 4.6 %collective-permute-start.4 = (f32[128,128]{1,0:T(8,128)S(1)}, f32[128,128]{1,0:T(8,128)S(1)}, u32[]{:S(2)}, u32[]{:S(2)}) collective-permute-start(f32[128,128]{1,0:T(8,128)S(1)} %get-tuple-element.23.own_ref), channel_id=1, source_target_pairs={{0,3},{1,2},{2,1},{3,0},{4,7},{5,6},{6,5},{7,4},{8,11},{9,10},{10,... | collective-permute-start | bytes 196616 | tf_op jit(solution)/shard_map/ppermute | solution.py:340
  45.6 2.3 %collective-permute-start.3 = (f32[128,128]{1,0:T(8,128)S(1)}, f32[128,128]{1,0:T(8,128)S(1)}, u32[]{:S(2)}, u32[]{:S(2)}) collective-permute-start(f32[128,128]{1,0:T(8,128)S(1)} %get-tuple-element.23.own_ref), channel_id=1, source_target_pairs={{0,2},{1,3},{2,0},{3,1},{4,6},{5,7},{6,4},{7,5},{8,10},{9,11},{10,... | collective-permute-start | bytes 196616 | tf_op jit(solution)/shard_map/ppermute | solution.py:340
  47.8 2.1 %collective-permute-start.2 = (f32[128,128]{1,0:T(8,128)S(1)}, f32[128,128]{1,0:T(8,128)S(1)}, u32[]{:S(2)}, u32[]{:S(2)}) collective-permute-start(f32[128,128]{1,0:T(8,128)S(1)} %get-tuple-element.23.own_ref), channel_id=1, source_target_pairs={{0,1},{1,0},{2,3},{3,2},{4,5},{5,4},{6,7},{7,6},{8,9},{9,8},{10,11... | collective-permute-start | bytes 196616 | tf_op jit(solution)/shard_map/ppermute | solution.py:340
  50.0 3.3 %collective-permute-start = (f32[32,128]{1,0:T(8,128)S(1)}, f32[32,128]{1,0:T(8,128)S(1)}, u32[]{:S(2)}, u32[]{:S(2)}) collective-permute-start(f32[32,128]{1,0:T(8,128)S(1)} %get-tuple-element.19), channel_id=1, source_target_pairs={{0,32},{32,64},{64,96},{96,128},{128,160},{160,192},{192,224},{224... | collective-permute-start | bytes 49160 | tf_op jit(solution)/shard_map/ppermute | solution.py:362
  53.3 1.4 %collective-permute-start.1 = (f32[32,128]{1,0:T(8,128)S(1)}, f32[32,128]{1,0:T(8,128)S(1)}, u32[]{:S(2)}, u32[]{:S(2)}) collective-permute-start(f32[32,128]{1,0:T(8,128)S(1)} %get-tuple-element.20), channel_id=1, source_target_pairs={{32,0},{64,32},{96,64},{128,96},{160,128},{192,160},{224,192},{256... | collective-permute-start | bytes 49160 | tf_op jit(solution)/shard_map/ppermute | solution.py:363
  54.7 0.2 shard_map.127.after_two.inverse_ref
  55.0 5.0 %collective-permute-done.1.high_ref = f32[32,128]{1,0:T(8,128)S(1)} collective-permute-done((f32[32,128]{1,0:T(8,128)S(1)}, f32[32,128]{1,0:T(8,128)S(1)}, u32[]{:S(2)}, u32[]{:S(2)}) %collective-permute-start.1) | collective-permute-done | bytes 16416 | tf_op jit(solution)/shard_map/ppermute | solution.py:363
  60.0 0.8 shard_map.125.near_ref
  60.8 1.1 shard_map.126.after_one.op_z_ref
  61.9 0.3 shard_map.128
  62.1 0.0 copy-start.10
  62.1 25.0 %all_to_all.21.recv_ref = f32[32,40,128]{2,1,0:T(8,128)S(1)} all-to-all(f32[32,40,128]{2,1,0:T(8,128)S(1)} %bitcast.17), channel_id=1, replica_groups=mesh['gx'=16,'gy'=8,'gz'=4] {'gz','gy'}, dimensions={0} | all-to-all | bytes 1310720 | tf_op jit(solution)/shard_map/all_to_all | solution.py:289
  87.2 2.5 %shard_map.129 = (f32[640,128]{1,0:T(8,128)S(1)}, f32[1,512]{1,0:T(1,128)}) custom-call(f32[32,40,128]{2,1,0:T(8,128)S(1)} %all_to_all.21.recv_ref, bf16[2,512,512]{2,1,0:T(8,128)(2,1)S(1)} %shard_map.126.after_one.op_z_ref, f32[4,128]{1,0:T(4,128)S(1)} %bitcast.30, bf16[2,512,512]{2,1,0:T(8,128)(2,1)S(1)} %shard_map.127.after_two.inverse_ref), custom_call_target="tpu_custom_call" | custom-call | flops 1000000 | bytes 100000 | tf_op jit(solution)/shard_map/pallas_call | solution.py:70
  89.6 14.8 %all_to_all.22 = f32[32,20,1,128]{3,2,1,0:T(1,128)S(1)} all-to-all(f32[32,20,1,128]{3,2,1,0:T(1,128)S(1)} %bitcast.19), channel_id=1, replica_groups=mesh['gx'=16,'gy'=8,'gz'=4] {'gz','gy'}, dimensions={0} | all-to-all | bytes 655360 | tf_op jit(solution)/shard_map/all_to_all | solution.py:289
  104.4 1.6 %shard_map.130 = f32[8,16,128]{2,1,0:T(8,128)} custom-call(f32[640,128]{1,0:T(8,128)S(1)} %bitcast.16, f32[128,128]{1,0:T(8,128)S(1)} %get-tuple-element.26.first_ref, s32[4,512]{1,0:T(4,128)S(1)} %bitcast.23, f32[4,512]{1,0:T(4,128)S(1)} %bitcast.25, s32[1,512]{1,0:T(1,128)S(1)} %bitcast.27, s32[1,512]{1,0:T(1,128)S(1)} %bitcast.29), custom_call_target="tpu_custom_call" | custom-call | flops 1000000 | bytes 100000 | tf_op jit(solution)/shard_map/pallas_call | solution.py:70
  (22 shorter events, 0.1 us)
Async XLA Ops:
  0.6 54.1 %copy-start = (f32[512,512]{1,0:T(8,128)S(1)}, f32[512,512]{1,0:T(8,128)}, u32[]{:S(2)}) copy-start(f32[512,512]{1,0:T(8,128)} %value_hbm.1) | copy-start | bytes 3145732
  32.4 6.8 %copy-start.1 = (f32[128,128]{1,0:T(8,128)S(1)}, f32[128,128]{1,0:T(8,128)}, u32[]{:S(2)}) copy-start(f32[128,128]{1,0:T(8,128)} %get-tuple-element.17.table_ref) | copy-start | bytes 196612
  32.4 6.8 %copy-start.3 = (f32[128,128]{1,0:T(8,128)S(1)}, f32[128,128]{1,0:T(8,128)}, u32[]{:S(2)}) copy-start(f32[128,128]{1,0:T(8,128)} %inv_z_in.1) | copy-start | bytes 196612
  32.4 6.8 %copy-start.5 = (f32[512,4]{0,1:T(4,128)S(1)}, f32[512,4]{0,1:T(4,128)}, u32[]{:S(2)}) copy-start(f32[512,4]{0,1:T(4,128)} %param.17) | copy-start | bytes 24580
  32.4 6.8 %copy-start.8 = (s32[512]{0:T(512)S(1)}, s32[512]{0:T(512)}, u32[]{:S(2)}) copy-start(s32[512]{0:T(512)} %param.19) | copy-start | bytes 6148
  32.4 6.8 %copy-start.9 = (f32[16,16]{1,0:T(8,128)S(1)}, f32[16,16]{1,0:T(8,128)}, u32[]{:S(2)}) copy-start(f32[16,16]{1,0:T(8,128)} %inv_y_ref.1) | copy-start | bytes 3076
  32.4 29.5 %all-to-all-start.1 = ((f32[16,56,128]{2,1,0:T(8,128)}), f32[16,56,128]{2,1,0:T(8,128)S(1)}, u32[]{:S(2)}, u32[]{:S(2)}) async-start(f32[16,56,128]{2,1,0:T(8,128)} %bitcast.4), calls=%async_computation.1 | async-start | bytes 917504 | tf_op jit(solution)/shard_map/all_to_all | solution.py:289
  39.1 0.7 copy-start.4
  39.1 0.7 copy-start.7
  40.9 19.8 %collective-permute-start.4 = (f32[128,128]{1,0:T(8,128)S(1)}, f32[128,128]{1,0:T(8,128)S(1)}, u32[]{:S(2)}, u32[]{:S(2)}) collective-permute-start(f32[128,128]{1,0:T(8,128)S(1)} %get-tuple-element.23.own_ref), channel_id=1, source_target_pairs={{0,3},{1,2},{2,1},{3,0},{4,7},{5,6},{6,5},{7,4},{8,11},{9,10},{10,... | collective-permute-start | bytes 196616 | tf_op jit(solution)/shard_map/ppermute | solution.py:340
  45.6 15.2 %collective-permute-start.3 = (f32[128,128]{1,0:T(8,128)S(1)}, f32[128,128]{1,0:T(8,128)S(1)}, u32[]{:S(2)}, u32[]{:S(2)}) collective-permute-start(f32[128,128]{1,0:T(8,128)S(1)} %get-tuple-element.23.own_ref), channel_id=1, source_target_pairs={{0,2},{1,3},{2,0},{3,1},{4,6},{5,7},{6,4},{7,5},{8,10},{9,11},{10,... | collective-permute-start | bytes 196616 | tf_op jit(solution)/shard_map/ppermute | solution.py:340
  47.8 12.9 %collective-permute-start.2 = (f32[128,128]{1,0:T(8,128)S(1)}, f32[128,128]{1,0:T(8,128)S(1)}, u32[]{:S(2)}, u32[]{:S(2)}) collective-permute-start(f32[128,128]{1,0:T(8,128)S(1)} %get-tuple-element.23.own_ref), channel_id=1, source_target_pairs={{0,1},{1,0},{2,3},{3,2},{4,5},{5,4},{6,7},{7,6},{8,9},{9,8},{10,11... | collective-permute-start | bytes 196616 | tf_op jit(solution)/shard_map/ppermute | solution.py:340
  50.0 5.0 %collective-permute-start = (f32[32,128]{1,0:T(8,128)S(1)}, f32[32,128]{1,0:T(8,128)S(1)}, u32[]{:S(2)}, u32[]{:S(2)}) collective-permute-start(f32[32,128]{1,0:T(8,128)S(1)} %get-tuple-element.19), channel_id=1, source_target_pairs={{0,32},{32,64},{64,96},{96,128},{128,160},{160,192},{192,224},{224... | collective-permute-start | bytes 49160 | tf_op jit(solution)/shard_map/ppermute | solution.py:362
  53.3 6.7 %copy-start.2 = (f32[8,16,128]{2,1,0:T(8,128)S(1)}, f32[8,16,128]{2,1,0:T(8,128)}, u32[]{:S(2)}) copy-start(f32[8,16,128]{2,1,0:T(8,128)} %param.12) | copy-start | bytes 196612
  53.3 6.7 %copy-start.6 = (f32[8,8]{1,0:T(8,128)S(1)}, f32[8,8]{1,0:T(8,128)}, u32[]{:S(2)}) copy-start(f32[8,8]{1,0:T(8,128)} %inv_ref.1) | copy-start | bytes 772
  53.3 6.7 %collective-permute-start.1 = (f32[32,128]{1,0:T(8,128)S(1)}, f32[32,128]{1,0:T(8,128)S(1)}, u32[]{:S(2)}, u32[]{:S(2)}) collective-permute-start(f32[32,128]{1,0:T(8,128)S(1)} %get-tuple-element.20), channel_id=1, source_target_pairs={{32,0},{64,32},{96,64},{128,96},{160,128},{192,160},{224,192},{256... | collective-permute-start | bytes 49160 | tf_op jit(solution)/shard_map/ppermute | solution.py:363
  62.1 25.0 %copy-start.10 = (f32[512]{0:T(512)S(1)}, f32[512]{0:T(512)}, u32[]{:S(2)}) copy-start(f32[512]{0:T(512)} %param.21) | copy-start | bytes 6148

commit v2 on v1

--- a/solution.py
+++ b/solution.py
@@ -86,9 +86,18 @@
         c.wait()
 
 
-def wide_dot(a, b):
+def stack_left(a):
+    high, low = split2(a)
+    zero = jnp.zeros(low.shape, BF16)
+    return jnp.concatenate(
+        [jnp.concatenate([high, high], axis=1), jnp.concatenate([low, zero], axis=1)], axis=0
+    )
+
+
+def wide_dot(left, b):
     high, low = split2(b)
-    return narrow_dot(a[0], high) + (narrow_dot(a[0], low) + narrow_dot(a[1], high))
+    both = narrow_dot(left, jnp.concatenate([high, low], axis=0))
+    return both[0:128] + both[128:256]
 
 
 def put_split(ref, cols, value):
@@ -130,11 +139,11 @@
     def store(k, value):
         power[:, 256 * k : 256 * k + value.shape[1]] = value
 
-    both = wide_dot(split2(op), jnp.concatenate([op, power[:, 0:256]], axis=1))
+    both = wide_dot(stack_left(op), jnp.concatenate([op, power[:, 0:256]], axis=1))
     store(1, both[:, 128:])
-    both = wide_dot(split2(both[:, 0:128]), jnp.concatenate([both[:, 0:128], power[:, 0:512]], axis=1))
+    both = wide_dot(stack_left(both[:, 0:128]), jnp.concatenate([both[:, 0:128], power[:, 0:512]], axis=1))
     store(2, both[:, 128:])
-    four = split2(both[:, 0:128])
+    four = stack_left(both[:, 0:128])
     store(4, wide_dot(four, power[:, 0:1024]))
     store(8, wide_dot(four, power[:, 1024 : 1024 + 128]))
     for m in range(SWEEPS - 1):
@@ -229,8 +238,9 @@
         highs.append(high)
         rests.append(rest)
     hot = jnp.concatenate(hots, axis=1)
-    total = narrow_dot(hot, jnp.concatenate(highs, axis=1), ((1,), (1,)))
-    total = total + narrow_dot(hot, jnp.concatenate(rests, axis=1), ((1,), (1,)))
+    values = jnp.concatenate([jnp.concatenate(highs, axis=1), jnp.concatenate(rests, axis=1)], axis=0)
+    both = narrow_dot(hot, values, ((1,), (1,)))
+    total = both[:, 0:128] + both[:, 128:256]
     for i in range(8):
         parts = [recv_ref[20 * o : 20 * o + 16, :] for o in range(4 * i, 4 * i + 4)]
         part = (parts[0] + parts[1]) + (parts[2] + parts[3])
@@ -254,14 +264,28 @@
         low[16 * y : 16 * y + 16, 128 * z : 128 * (z + 1)] = recv_ref[o, 0:16]
         acc[16 * y : 16 * y + 16, 128 * z : 128 * (z + 1)] = recv_ref[o, 16:32]
         op_y[16 * y + 4 * z : 16 * y + 4 * z + 4, :] = recv_ref[o, 36:40]
-    y_high, y_low = split2(op_y[...])
-    y_both = jnp.concatenate([y_high, y_high], axis=1)
+    y_left = stack_left(op_y[...])
+
+    right = op_z_ref[0, 240:256, 256:384].astype(F32) + op_z_ref[1, 240:256, 256:384].astype(F32)
+    left = op_z_ref[0, 256:272, 128:256].astype(F32) + op_z_ref[1, 256:272, 128:256].astype(F32)
 
     def apply():
-        high, rest = split2(acc[...])
-        along_y = narrow_dot(y_both, jnp.concatenate([high, rest], axis=0)) + narrow_dot(y_low, high)
-        along_z = narrow_dot(high, op_z_ref[0]) + (narrow_dot(high, op_z_ref[1]) + narrow_dot(rest, op_z_ref[0]))
-        return along_y + along_z
+        v = acc[...]
+        high, rest = split2(v)
+        both = jnp.concatenate([high, rest], axis=0)
+        y = narrow_dot(y_left, both)
+        y = y[0:128] + y[128:256]
+        halves = []
+        for n in range(2):
+            part = slice(256 * n, 256 * n + 256)
+            z = narrow_dot(both[:, part], op_z_ref[0, part, part])
+            halves.append(y[:, part] + (z[0:128] + z[128:256]) + narrow_dot(high[:, part], op_z_ref[1, part, part]))
+        to_right = v[:, 254:255] * right[14:15] + v[:, 255:256] * right[15:16]
+        to_left = v[:, 256:257] * left[0:1] + v[:, 257:258] * left[1:2]
+        return jnp.concatenate(
+            [halves[0][:, 0:128], halves[0][:, 128:256] + to_left, halves[1][:, 0:128] + to_right, halves[1][:, 128:256]],
+            axis=1,
+        )
 
     heat = jnp.sum(recv_ref[:, 32:40, :], axis=0)[0:4, :] + source_ref[...]
     high, rest = split2(jnp.concatenate([heat[h : h + 1, :] for h in range(4)], axis=1))

time: 107 us -> 106 us (level)
  no operation moved by 1% of the time
where the time goes in v2:
time: 106 us; the launch traced here: 105 us
  blocking collectives  67.3 us (63%)
  starting transfers between devices  20.5 us (19%)
  Pallas kernels  10.7 us (10%)
  waiting for transfers between devices  5.02 us (5%)
    all_to_all x3, blocking collectives, exchange(): return lax.all_to_all(v, axes, split_axis=0, concat_axis=0, tiled=True)  67.3 us
    pallas_call x9, Pallas kernels, call(): pl.pallas_call(body, out_shape=outs, in_specs=[VM] * len(args) if specs i...  10.7 us
    ppermute x3, starting transfers between devices, shards(): lax.ppermute(inv_z, 'gz', [(i, i ^ d) for i in range(4)])  9.06 us
    all_to_all x1, starting transfers between devices, exchange(): return lax.all_to_all(v, axes, split_axis=0, concat_axis=0, tiled=True)  6.72 us
    ppermute x1, waiting for transfers between devices, shards(): lax.ppermute(low, 'gx', [(j, i) for i, j in up])  5.01 us
    ppermute x1, starting transfers between devices, shards(): lax.ppermute(high, 'gx', up)  3.25 us
  transfers between devices with their start and end apart: 6, of which 1 were waited for; matrix products, arithmetic and copies ran while one was open for 0% of the time, Pallas kernels for 3%

profile of v2, /device:TPU:1, one launch (start us, length us, event | category | flops | bytes accessed | tf_op | source)
XLA Modules:
  0.0 105.0 jit_solution(5453368515423262324)
XLA Ops:
  0.6 1.7 %shard_map.122 = (f32[272,128]{1,0:T(8,128)}, f32[128,128]{1,0:T(8,128)}) custom-call(f32[128,128]{1,0:T(8,128)} %bitcast.32, f32[128,128]{1,0:T(8,128)} %bitcast.20, f32[8,8]{1,0:T(8,128)} %inv_ref.1), custom_call_target="tpu_custom_call" | custom-call | flops 1000000 | bytes 100000 | tf_op jit(solution)/shard_map/pallas_call | solution.py:70
  2.4 27.8 %all_to_all.20 = f32[16,17,1,128]{3,2,1,0:T(1,128)S(1)} all-to-all(f32[16,17,1,128]{3,2,1,0:T(1,128)} %bitcast.31), channel_id=1, replica_groups=mesh['gx'=16,'gy'=8,'gz'=4] {'gx'}, dimensions={0} | all-to-all | bytes 278528 | tf_op jit(solution)/shard_map/all_to_all | solution.py:313
  30.2 2.0 %shard_map.123 = (f32[896,128]{1,0:T(8,128)}, f32[8,128]{1,0:T(8,128)S(1)}) custom-call(f32[272,128]{1,0:T(8,128)S(1)} %bitcast.18), custom_call_target="tpu_custom_call" | custom-call | flops 1000000 | bytes 100000 | tf_op jit(solution)/shard_map/pallas_call | solution.py:70
  32.2 0.0 copy-start.9
  32.2 6.7 %all-to-all-start.1 = ((f32[16,56,128]{2,1,0:T(8,128)}), f32[16,56,128]{2,1,0:T(8,128)S(1)}, u32[]{:S(2)}, u32[]{:S(2)}) async-start(f32[16,56,128]{2,1,0:T(8,128)} %bitcast.4), calls=%async_computation.1 | async-start | bytes 917504 | tf_op jit(solution)/shard_map/all_to_all | solution.py:313
  38.9 0.0 copy-start.4
  39.0 0.0 copy-start.7
  39.0 0.6 copy-done.4
  39.7 1.1 %shard_map.124 = (f32[128,128]{1,0:T(8,128)S(1)}, f32[8,128]{1,0:T(8,128)S(1)}, f32[128,128]{1,0:T(8,128)S(1)}, f32[32,128]{1,0:T(8,128)S(1)}, f32[32,128]{1,0:T(8,128)S(1)}) custom-call(f32[128,128]{1,0:T(8,128)S(1)} %copy-done.1, s32[4,512]{1,0:T(4,128)S(1)} %bitcast.22, f32[4,512]{1,0:T(4,128)S(1)} %bitcast.24, s32[1,512]{1,0:T(1,128)S(1)} %bitcast.26, ...), custom_call_target="tpu_custom_call" | custom-call | flops 1000000 | bytes 100000 | tf_op jit(solution)/shard_map/pallas_call | solution.py:70
  40.7 4.7 %collective-permute-start.4 = (f32[128,128]{1,0:T(8,128)S(1)}, f32[128,128]{1,0:T(8,128)S(1)}, u32[]{:S(2)}, u32[]{:S(2)}) collective-permute-start(f32[128,128]{1,0:T(8,128)S(1)} %get-tuple-element.23.own_ref), channel_id=1, source_target_pairs={{0,3},{1,2},{2,1},{3,0},{4,7},{5,6},{6,5},{7,4},{8,11},{9,10},{10,... | collective-permute-start | bytes 196616 | tf_op jit(solution)/shard_map/ppermute | solution.py:364
  45.4 2.2 %collective-permute-start.3 = (f32[128,128]{1,0:T(8,128)S(1)}, f32[128,128]{1,0:T(8,128)S(1)}, u32[]{:S(2)}, u32[]{:S(2)}) collective-permute-start(f32[128,128]{1,0:T(8,128)S(1)} %get-tuple-element.23.own_ref), channel_id=1, source_target_pairs={{0,2},{1,3},{2,0},{3,1},{4,6},{5,7},{6,4},{7,5},{8,10},{9,11},{10,... | collective-permute-start | bytes 196616 | tf_op jit(solution)/shard_map/ppermute | solution.py:364
  47.7 2.2 %collective-permute-start.2 = (f32[128,128]{1,0:T(8,128)S(1)}, f32[128,128]{1,0:T(8,128)S(1)}, u32[]{:S(2)}, u32[]{:S(2)}) collective-permute-start(f32[128,128]{1,0:T(8,128)S(1)} %get-tuple-element.23.own_ref), channel_id=1, source_target_pairs={{0,1},{1,0},{2,3},{3,2},{4,5},{5,4},{6,7},{7,6},{8,9},{9,8},{10,11... | collective-permute-start | bytes 196616 | tf_op jit(solution)/shard_map/ppermute | solution.py:364
  49.8 3.3 %collective-permute-start = (f32[32,128]{1,0:T(8,128)S(1)}, f32[32,128]{1,0:T(8,128)S(1)}, u32[]{:S(2)}, u32[]{:S(2)}) collective-permute-start(f32[32,128]{1,0:T(8,128)S(1)} %get-tuple-element.19), channel_id=1, source_target_pairs={{0,32},{32,64},{64,96},{96,128},{128,160},{160,192},{192,224},{224... | collective-permute-start | bytes 49160 | tf_op jit(solution)/shard_map/ppermute | solution.py:386
  53.1 0.0 copy-start.2
  53.1 1.4 %collective-permute-start.1 = (f32[32,128]{1,0:T(8,128)S(1)}, f32[32,128]{1,0:T(8,128)S(1)}, u32[]{:S(2)}, u32[]{:S(2)}) collective-permute-start(f32[32,128]{1,0:T(8,128)S(1)} %get-tuple-element.20), channel_id=1, source_target_pairs={{32,0},{64,32},{96,64},{128,96},{160,128},{192,160},{224,192},{256... | collective-permute-start | bytes 49160 | tf_op jit(solution)/shard_map/ppermute | solution.py:387
  54.5 0.2 shard_map.127.after_two.inverse_ref
  54.8 5.0 %collective-permute-done.1.high_ref = f32[32,128]{1,0:T(8,128)S(1)} collective-permute-done((f32[32,128]{1,0:T(8,128)S(1)}, f32[32,128]{1,0:T(8,128)S(1)}, u32[]{:S(2)}, u32[]{:S(2)}) %collective-permute-start.1) | collective-permute-done | bytes 16416 | tf_op jit(solution)/shard_map/ppermute | solution.py:387
  59.8 0.8 shard_map.125.near_ref
  60.6 1.1 %shard_map.126.after_one.op_z_ref = bf16[2,512,512]{2,1,0:T(8,128)(2,1)S(1)} custom-call(f32[128,128]{1,0:T(8,128)S(1)} %get-tuple-element.23.own_ref, f32[128,128]{1,0:T(8,128)S(1)} %collective-permute-done.2.one_ref, f32[128,128]{1,0:T(8,128)S(1)} %collective-permute-done.3.two_ref, f32[128,128]{1,0:T(8,128)S(1)} %collective-permute-done.4.three_ref), custom_call_target="tpu_custom_call" | custom-call | flops 1000000 | bytes 100000 | tf_op jit(solution)/shard_map/pallas_call | solution.py:70
  61.7 0.3 shard_map.128
  62.0 25.0 %all_to_all.21.recv_ref = f32[32,40,128]{2,1,0:T(8,128)S(1)} all-to-all(f32[32,40,128]{2,1,0:T(8,128)S(1)} %bitcast.17), channel_id=1, replica_groups=mesh['gx'=16,'gy'=8,'gz'=4] {'gz','gy'}, dimensions={0} | all-to-all | bytes 1310720 | tf_op jit(solution)/shard_map/all_to_all | solution.py:313
  87.0 2.1 %shard_map.129 = (f32[640,128]{1,0:T(8,128)S(1)}, f32[1,512]{1,0:T(1,128)}) custom-call(f32[32,40,128]{2,1,0:T(8,128)S(1)} %all_to_all.21.recv_ref, bf16[2,512,512]{2,1,0:T(8,128)(2,1)S(1)} %shard_map.126.after_one.op_z_ref, f32[4,128]{1,0:T(4,128)S(1)} %bitcast.30, bf16[2,512,512]{2,1,0:T(8,128)(2,1)S(1)} %shard_map.127.after_two.inverse_ref), custom_call_target="tpu_custom_call" | custom-call | flops 1000000 | bytes 100000 | tf_op jit(solution)/shard_map/pallas_call | solution.py:70
  89.1 14.5 %all_to_all.22 = f32[32,20,1,128]{3,2,1,0:T(1,128)S(1)} all-to-all(f32[32,20,1,128]{3,2,1,0:T(1,128)S(1)} %bitcast.19), channel_id=1, replica_groups=mesh['gx'=16,'gy'=8,'gz'=4] {'gz','gy'}, dimensions={0} | all-to-all | bytes 655360 | tf_op jit(solution)/shard_map/all_to_all | solution.py:313
  103.6 1.5 %shard_map.130 = f32[8,16,128]{2,1,0:T(8,128)} custom-call(f32[640,128]{1,0:T(8,128)S(1)} %bitcast.16, f32[128,128]{1,0:T(8,128)S(1)} %get-tuple-element.26.first_ref, s32[4,512]{1,0:T(4,128)S(1)} %bitcast.23, f32[4,512]{1,0:T(4,128)S(1)} %bitcast.25, s32[1,512]{1,0:T(1,128)S(1)} %bitcast.27, s32[1,512]{1,0:T(1,128)S(1)} %bitcast.29), custom_call_target="tpu_custom_call" | custom-call | flops 1000000 | bytes 100000 | tf_op jit(solution)/shard_map/pallas_call | solution.py:70
  (22 shorter events, 0.1 us)
Async XLA Ops:
  0.6 53.9 %copy-start = (f32[512,512]{1,0:T(8,128)S(1)}, f32[512,512]{1,0:T(8,128)}, u32[]{:S(2)}) copy-start(f32[512,512]{1,0:T(8,128)} %value_hbm.1) | copy-start | bytes 3145732
  32.2 6.8 %copy-start.1 = (f32[128,128]{1,0:T(8,128)S(1)}, f32[128,128]{1,0:T(8,128)}, u32[]{:S(2)}) copy-start(f32[128,128]{1,0:T(8,128)} %get-tuple-element.17.table_ref) | copy-start | bytes 196612
  32.2 6.8 %copy-start.3 = (f32[128,128]{1,0:T(8,128)S(1)}, f32[128,128]{1,0:T(8,128)}, u32[]{:S(2)}) copy-start(f32[128,128]{1,0:T(8,128)} %inv_z_in.1) | copy-start | bytes 196612
  32.2 6.8 %copy-start.5 = (f32[512,4]{0,1:T(4,128)S(1)}, f32[512,4]{0,1:T(4,128)}, u32[]{:S(2)}) copy-start(f32[512,4]{0,1:T(4,128)} %param.17) | copy-start | bytes 24580
  32.2 6.8 %copy-start.8 = (s32[512]{0:T(512)S(1)}, s32[512]{0:T(512)}, u32[]{:S(2)}) copy-start(s32[512]{0:T(512)} %param.19) | copy-start | bytes 6148
  32.2 6.8 %copy-start.9 = (f32[16,16]{1,0:T(8,128)S(1)}, f32[16,16]{1,0:T(8,128)}, u32[]{:S(2)}) copy-start(f32[16,16]{1,0:T(8,128)} %inv_y_ref.1) | copy-start | bytes 3076
  32.2 29.5 %all-to-all-start.1 = ((f32[16,56,128]{2,1,0:T(8,128)}), f32[16,56,128]{2,1,0:T(8,128)S(1)}, u32[]{:S(2)}, u32[]{:S(2)}) async-start(f32[16,56,128]{2,1,0:T(8,128)} %bitcast.4), calls=%async_computation.1 | async-start | bytes 917504 | tf_op jit(solution)/shard_map/all_to_all | solution.py:313
  38.9 0.7 copy-start.4
  39.0 0.7 copy-start.7
  40.7 19.8 %collective-permute-start.4 = (f32[128,128]{1,0:T(8,128)S(1)}, f32[128,128]{1,0:T(8,128)S(1)}, u32[]{:S(2)}, u32[]{:S(2)}) collective-permute-start(f32[128,128]{1,0:T(8,128)S(1)} %get-tuple-element.23.own_ref), channel_id=1, source_target_pairs={{0,3},{1,2},{2,1},{3,0},{4,7},{5,6},{6,5},{7,4},{8,11},{9,10},{10,... | collective-permute-start | bytes 196616 | tf_op jit(solution)/shard_map/ppermute | solution.py:364
  45.4 15.2 %collective-permute-start.3 = (f32[128,128]{1,0:T(8,128)S(1)}, f32[128,128]{1,0:T(8,128)S(1)}, u32[]{:S(2)}, u32[]{:S(2)}) collective-permute-start(f32[128,128]{1,0:T(8,128)S(1)} %get-tuple-element.23.own_ref), channel_id=1, source_target_pairs={{0,2},{1,3},{2,0},{3,1},{4,6},{5,7},{6,4},{7,5},{8,10},{9,11},{10,... | collective-permute-start | bytes 196616 | tf_op jit(solution)/shard_map/ppermute | solution.py:364
  47.7 13.0 %collective-permute-start.2 = (f32[128,128]{1,0:T(8,128)S(1)}, f32[128,128]{1,0:T(8,128)S(1)}, u32[]{:S(2)}, u32[]{:S(2)}) collective-permute-start(f32[128,128]{1,0:T(8,128)S(1)} %get-tuple-element.23.own_ref), channel_id=1, source_target_pairs={{0,1},{1,0},{2,3},{3,2},{4,5},{5,4},{6,7},{7,6},{8,9},{9,8},{10,11... | collective-permute-start | bytes 196616 | tf_op jit(solution)/shard_map/ppermute | solution.py:364
  49.8 5.0 %collective-permute-start = (f32[32,128]{1,0:T(8,128)S(1)}, f32[32,128]{1,0:T(8,128)S(1)}, u32[]{:S(2)}, u32[]{:S(2)}) collective-permute-start(f32[32,128]{1,0:T(8,128)S(1)} %get-tuple-element.19), channel_id=1, source_target_pairs={{0,32},{32,64},{64,96},{96,128},{128,160},{160,192},{192,224},{224... | collective-permute-start | bytes 49160 | tf_op jit(solution)/shard_map/ppermute | solution.py:386
  53.1 6.7 %copy-start.2 = (f32[8,16,128]{2,1,0:T(8,128)S(1)}, f32[8,16,128]{2,1,0:T(8,128)}, u32[]{:S(2)}) copy-start(f32[8,16,128]{2,1,0:T(8,128)} %param.12) | copy-start | bytes 196612
  53.1 6.7 %copy-start.6 = (f32[8,8]{1,0:T(8,128)S(1)}, f32[8,8]{1,0:T(8,128)}, u32[]{:S(2)}) copy-start(f32[8,8]{1,0:T(8,128)} %inv_ref.1) | copy-start | bytes 772
  53.1 6.7 %collective-permute-start.1 = (f32[32,128]{1,0:T(8,128)S(1)}, f32[32,128]{1,0:T(8,128)S(1)}, u32[]{:S(2)}, u32[]{:S(2)}) collective-permute-start(f32[32,128]{1,0:T(8,128)S(1)} %get-tuple-element.20), channel_id=1, source_target_pairs={{32,0},{64,32},{96,64},{128,96},{160,128},{192,160},{224,192},{256... | collective-permute-start | bytes 49160 | tf_op jit(solution)/shard_map/ppermute | solution.py:387
  62.0 25.0 %copy-start.10 = (f32[512]{0:T(512)S(1)}, f32[512]{0:T(512)}, u32[]{:S(2)}) copy-start(f32[512]{0:T(512)} %param.21) | copy-start | bytes 6148

commit v3 on v2

--- a/solution.py
+++ b/solution.py
@@ -269,8 +269,7 @@
     right = op_z_ref[0, 240:256, 256:384].astype(F32) + op_z_ref[1, 240:256, 256:384].astype(F32)
     left = op_z_ref[0, 256:272, 128:256].astype(F32) + op_z_ref[1, 256:272, 128:256].astype(F32)
 
-    def apply():
-        v = acc[...]
+    def apply(v):
         high, rest = split2(v)
         both = jnp.concatenate([high, rest], axis=0)
         y = narrow_dot(y_left, both)
@@ -297,13 +296,13 @@
     for o in range(32):
         out_ref[20 * o + 16 : 20 * o + 20, :] = rows
 
-    acc[...] = apply() + low[...]
-
-    def step(_, c):
-        acc[...] = apply()
-        return c
-
-    lax.fori_loop(0, 2 * q + 1, step, 0)
+    acc[...] = apply(apply(acc[...]) + low[...])
+    for pair in range(1, 4):
+
+        @pl.when(q >= pair)
+        def _():
+            acc[...] = apply(apply(acc[...]))
+
     for o in range(32):
         z, y = divmod(o, 8)
         out_ref[20 * o : 20 * o + 16, :] = acc[16 * y : 16 * y + 16, 128 * z : 128 * (z + 1)]

time: 106 us -> 106 us (level)
  no operation moved by 1% of the time
where the time goes in v3:
time: 106 us; the launch traced here: 105 us
  blocking collectives  67.2 us (63%)
  starting transfers between devices  20.5 us (19%)
  Pallas kernels  10.7 us (10%)
  waiting for transfers between devices  5.02 us (5%)
    all_to_all x3, blocking collectives, exchange(): return lax.all_to_all(v, axes, split_axis=0, concat_axis=0, tiled=True)  67.2 us
    pallas_call x9, Pallas kernels, call(): pl.pallas_call(body, out_shape=outs, in_specs=[VM] * len(args) if specs i...  10.7 us
    ppermute x3, starting transfers between devices, shards(): lax.ppermute(inv_z, 'gz', [(i, i ^ d) for i in range(4)])  9.06 us
    all_to_all x1, starting transfers between devices, exchange(): return lax.all_to_all(v, axes, split_axis=0, concat_axis=0, tiled=True)  6.72 us
    ppermute x1, waiting for transfers between devices, shards(): lax.ppermute(low, 'gx', [(j, i) for i, j in up])  5.01 us
    ppermute x1, starting transfers between devices, shards(): lax.ppermute(high, 'gx', up)  3.25 us
  transfers between devices with their start and end apart: 6, of which 1 were waited for; matrix products, arithmetic and copies ran while one was open for 0% of the time, Pallas kernels for 3%

profile of v3, /device:TPU:1, one launch (start us, length us, event | category | flops | bytes accessed | tf_op | source)
XLA Modules:
  0.0 105.0 jit_solution(6410197054077526552)
XLA Ops:
  0.6 1.7 %shard_map.122 = (f32[272,128]{1,0:T(8,128)}, f32[128,128]{1,0:T(8,128)}) custom-call(f32[128,128]{1,0:T(8,128)} %bitcast.32, f32[128,128]{1,0:T(8,128)} %bitcast.20, f32[8,8]{1,0:T(8,128)} %inv_ref.1), custom_call_target="tpu_custom_call" | custom-call | flops 1000000 | bytes 100000 | tf_op jit(solution)/shard_map/pallas_call | solution.py:70
  2.4 27.8 %all_to_all.20 = f32[16,17,1,128]{3,2,1,0:T(1,128)S(1)} all-to-all(f32[16,17,1,128]{3,2,1,0:T(1,128)} %bitcast.31), channel_id=1, replica_groups=mesh['gx'=16,'gy'=8,'gz'=4] {'gx'}, dimensions={0} | all-to-all | bytes 278528 | tf_op jit(solution)/shard_map/all_to_all | solution.py:312
  30.2 2.0 %shard_map.123 = (f32[896,128]{1,0:T(8,128)}, f32[8,128]{1,0:T(8,128)S(1)}) custom-call(f32[272,128]{1,0:T(8,128)S(1)} %bitcast.18), custom_call_target="tpu_custom_call" | custom-call | flops 1000000 | bytes 100000 | tf_op jit(solution)/shard_map/pallas_call | solution.py:70
  32.2 0.0 copy-start.9
  32.2 6.7 %all-to-all-start.1 = ((f32[16,56,128]{2,1,0:T(8,128)}), f32[16,56,128]{2,1,0:T(8,128)S(1)}, u32[]{:S(2)}, u32[]{:S(2)}) async-start(f32[16,56,128]{2,1,0:T(8,128)} %bitcast.4), calls=%async_computation.1 | async-start | bytes 917504 | tf_op jit(solution)/shard_map/all_to_all | solution.py:312
  38.9 0.0 copy-start.4
  39.0 0.0 copy-start.7
  39.0 0.6 copy-done.4
  39.7 1.1 %shard_map.124 = (f32[128,128]{1,0:T(8,128)S(1)}, f32[8,128]{1,0:T(8,128)S(1)}, f32[128,128]{1,0:T(8,128)S(1)}, f32[32,128]{1,0:T(8,128)S(1)}, f32[32,128]{1,0:T(8,128)S(1)}) custom-call(f32[128,128]{1,0:T(8,128)S(1)} %copy-done.1, s32[4,512]{1,0:T(4,128)S(1)} %bitcast.22, f32[4,512]{1,0:T(4,128)S(1)} %bitcast.24, s32[1,512]{1,0:T(1,128)S(1)} %bitcast.26, ...), custom_call_target="tpu_custom_call" | custom-call | flops 1000000 | bytes 100000 | tf_op jit(solution)/shard_map/pallas_call | solution.py:70
  40.7 4.7 %collective-permute-start.4 = (f32[128,128]{1,0:T(8,128)S(1)}, f32[128,128]{1,0:T(8,128)S(1)}, u32[]{:S(2)}, u32[]{:S(2)}) collective-permute-start(f32[128,128]{1,0:T(8,128)S(1)} %get-tuple-element.23.own_ref), channel_id=1, source_target_pairs={{0,3},{1,2},{2,1},{3,0},{4,7},{5,6},{6,5},{7,4},{8,11},{9,10},{10,... | collective-permute-start | bytes 196616 | tf_op jit(solution)/shard_map/ppermute | solution.py:363
  45.4 2.2 %collective-permute-start.3 = (f32[128,128]{1,0:T(8,128)S(1)}, f32[128,128]{1,0:T(8,128)S(1)}, u32[]{:S(2)}, u32[]{:S(2)}) collective-permute-start(f32[128,128]{1,0:T(8,128)S(1)} %get-tuple-element.23.own_ref), channel_id=1, source_target_pairs={{0,2},{1,3},{2,0},{3,1},{4,6},{5,7},{6,4},{7,5},{8,10},{9,11},{10,... | collective-permute-start | bytes 196616 | tf_op jit(solution)/shard_map/ppermute | solution.py:363
  47.7 2.2 %collective-permute-start.2 = (f32[128,128]{1,0:T(8,128)S(1)}, f32[128,128]{1,0:T(8,128)S(1)}, u32[]{:S(2)}, u32[]{:S(2)}) collective-permute-start(f32[128,128]{1,0:T(8,128)S(1)} %get-tuple-element.23.own_ref), channel_id=1, source_target_pairs={{0,1},{1,0},{2,3},{3,2},{4,5},{5,4},{6,7},{7,6},{8,9},{9,8},{10,11... | collective-permute-start | bytes 196616 | tf_op jit(solution)/shard_map/ppermute | solution.py:363
  49.8 3.3 %collective-permute-start = (f32[32,128]{1,0:T(8,128)S(1)}, f32[32,128]{1,0:T(8,128)S(1)}, u32[]{:S(2)}, u32[]{:S(2)}) collective-permute-start(f32[32,128]{1,0:T(8,128)S(1)} %get-tuple-element.19), channel_id=1, source_target_pairs={{0,32},{32,64},{64,96},{96,128},{128,160},{160,192},{192,224},{224... | collective-permute-start | bytes 49160 | tf_op jit(solution)/shard_map/ppermute | solution.py:385
  53.1 0.0 copy-start.2
  53.1 1.4 %collective-permute-start.1 = (f32[32,128]{1,0:T(8,128)S(1)}, f32[32,128]{1,0:T(8,128)S(1)}, u32[]{:S(2)}, u32[]{:S(2)}) collective-permute-start(f32[32,128]{1,0:T(8,128)S(1)} %get-tuple-element.20), channel_id=1, source_target_pairs={{32,0},{64,32},{96,64},{128,96},{160,128},{192,160},{224,192},{256... | collective-permute-start | bytes 49160 | tf_op jit(solution)/shard_map/ppermute | solution.py:386
  54.5 0.2 shard_map.127.after_two.inverse_ref
  54.8 5.0 %collective-permute-done.1.high_ref = f32[32,128]{1,0:T(8,128)S(1)} collective-permute-done((f32[32,128]{1,0:T(8,128)S(1)}, f32[32,128]{1,0:T(8,128)S(1)}, u32[]{:S(2)}, u32[]{:S(2)}) %collective-permute-start.1) | collective-permute-done | bytes 16416 | tf_op jit(solution)/shard_map/ppermute | solution.py:386
  59.8 0.8 shard_map.125.near_ref
  60.6 1.1 %shard_map.126.after_one.op_z_ref = bf16[2,512,512]{2,1,0:T(8,128)(2,1)S(1)} custom-call(f32[128,128]{1,0:T(8,128)S(1)} %get-tuple-element.23.own_ref, f32[128,128]{1,0:T(8,128)S(1)} %collective-permute-done.2.one_ref, f32[128,128]{1,0:T(8,128)S(1)} %collective-permute-done.3.two_ref, f32[128,128]{1,0:T(8,128)S(1)} %collective-permute-done.4.three_ref), custom_call_target="tpu_custom_call" | custom-call | flops 1000000 | bytes 100000 | tf_op jit(solution)/shard_map/pallas_call | solution.py:70
  61.7 0.3 shard_map.128
  62.0 25.0 %all_to_all.21.recv_ref = f32[32,40,128]{2,1,0:T(8,128)S(1)} all-to-all(f32[32,40,128]{2,1,0:T(8,128)S(1)} %bitcast.17), channel_id=1, replica_groups=mesh['gx'=16,'gy'=8,'gz'=4] {'gz','gy'}, dimensions={0} | all-to-all | bytes 1310720 | tf_op jit(solution)/shard_map/all_to_all | solution.py:312
  87.0 2.1 %shard_map.129 = (f32[640,128]{1,0:T(8,128)S(1)}, f32[1,512]{1,0:T(1,128)}) custom-call(f32[32,40,128]{2,1,0:T(8,128)S(1)} %all_to_all.21.recv_ref, bf16[2,512,512]{2,1,0:T(8,128)(2,1)S(1)} %shard_map.126.after_one.op_z_ref, f32[4,128]{1,0:T(4,128)S(1)} %bitcast.30, bf16[2,512,512]{2,1,0:T(8,128)(2,1)S(1)} %shard_map.127.after_two.inverse_ref), custom_call_target="tpu_custom_call" | custom-call | flops 1000000 | bytes 100000 | tf_op jit(solution)/shard_map/pallas_call | solution.py:70
  89.1 14.4 %all_to_all.22 = f32[32,20,1,128]{3,2,1,0:T(1,128)S(1)} all-to-all(f32[32,20,1,128]{3,2,1,0:T(1,128)S(1)} %bitcast.19), channel_id=1, replica_groups=mesh['gx'=16,'gy'=8,'gz'=4] {'gz','gy'}, dimensions={0} | all-to-all | bytes 655360 | tf_op jit(solution)/shard_map/all_to_all | solution.py:312
  103.5 1.5 %shard_map.130 = f32[8,16,128]{2,1,0:T(8,128)} custom-call(f32[640,128]{1,0:T(8,128)S(1)} %bitcast.16, f32[128,128]{1,0:T(8,128)S(1)} %get-tuple-element.26.first_ref, s32[4,512]{1,0:T(4,128)S(1)} %bitcast.23, f32[4,512]{1,0:T(4,128)S(1)} %bitcast.25, s32[1,512]{1,0:T(1,128)S(1)} %bitcast.27, s32[1,512]{1,0:T(1,128)S(1)} %bitcast.29), custom_call_target="tpu_custom_call" | custom-call | flops 1000000 | bytes 100000 | tf_op jit(solution)/shard_map/pallas_call | solution.py:70
  (22 shorter events, 0.1 us)
Async XLA Ops:
  0.6 53.9 %copy-start = (f32[512,512]{1,0:T(8,128)S(1)}, f32[512,512]{1,0:T(8,128)}, u32[]{:S(2)}) copy-start(f32[512,512]{1,0:T(8,128)} %value_hbm.1) | copy-start | bytes 3145732
  32.2 6.8 %copy-start.1 = (f32[128,128]{1,0:T(8,128)S(1)}, f32[128,128]{1,0:T(8,128)}, u32[]{:S(2)}) copy-start(f32[128,128]{1,0:T(8,128)} %get-tuple-element.17.table_ref) | copy-start | bytes 196612
  32.2 6.8 %copy-start.3 = (f32[128,128]{1,0:T(8,128)S(1)}, f32[128,128]{1,0:T(8,128)}, u32[]{:S(2)}) copy-start(f32[128,128]{1,0:T(8,128)} %inv_z_in.1) | copy-start | bytes 196612
  32.2 6.8 %copy-start.5 = (f32[512,4]{0,1:T(4,128)S(1)}, f32[512,4]{0,1:T(4,128)}, u32[]{:S(2)}) copy-start(f32[512,4]{0,1:T(4,128)} %param.17) | copy-start | bytes 24580
  32.2 6.8 %copy-start.8 = (s32[512]{0:T(512)S(1)}, s32[512]{0:T(512)}, u32[]{:S(2)}) copy-start(s32[512]{0:T(512)} %param.19) | copy-start | bytes 6148
  32.2 6.8 %copy-start.9 = (f32[16,16]{1,0:T(8,128)S(1)}, f32[16,16]{1,0:T(8,128)}, u32[]{:S(2)}) copy-start(f32[16,16]{1,0:T(8,128)} %inv_y_ref.1) | copy-start | bytes 3076
  32.2 29.5 %all-to-all-start.1 = ((f32[16,56,128]{2,1,0:T(8,128)}), f32[16,56,128]{2,1,0:T(8,128)S(1)}, u32[]{:S(2)}, u32[]{:S(2)}) async-start(f32[16,56,128]{2,1,0:T(8,128)} %bitcast.4), calls=%async_computation.1 | async-start | bytes 917504 | tf_op jit(solution)/shard_map/all_to_all | solution.py:312
  38.9 0.7 copy-start.4
  39.0 0.7 copy-start.7
  40.7 19.8 %collective-permute-start.4 = (f32[128,128]{1,0:T(8,128)S(1)}, f32[128,128]{1,0:T(8,128)S(1)}, u32[]{:S(2)}, u32[]{:S(2)}) collective-permute-start(f32[128,128]{1,0:T(8,128)S(1)} %get-tuple-element.23.own_ref), channel_id=1, source_target_pairs={{0,3},{1,2},{2,1},{3,0},{4,7},{5,6},{6,5},{7,4},{8,11},{9,10},{10,... | collective-permute-start | bytes 196616 | tf_op jit(solution)/shard_map/ppermute | solution.py:363
  45.4 15.2 %collective-permute-start.3 = (f32[128,128]{1,0:T(8,128)S(1)}, f32[128,128]{1,0:T(8,128)S(1)}, u32[]{:S(2)}, u32[]{:S(2)}) collective-permute-start(f32[128,128]{1,0:T(8,128)S(1)} %get-tuple-element.23.own_ref), channel_id=1, source_target_pairs={{0,2},{1,3},{2,0},{3,1},{4,6},{5,7},{6,4},{7,5},{8,10},{9,11},{10,... | collective-permute-start | bytes 196616 | tf_op jit(solution)/shard_map/ppermute | solution.py:363
  47.7 13.0 %collective-permute-start.2 = (f32[128,128]{1,0:T(8,128)S(1)}, f32[128,128]{1,0:T(8,128)S(1)}, u32[]{:S(2)}, u32[]{:S(2)}) collective-permute-start(f32[128,128]{1,0:T(8,128)S(1)} %get-tuple-element.23.own_ref), channel_id=1, source_target_pairs={{0,1},{1,0},{2,3},{3,2},{4,5},{5,4},{6,7},{7,6},{8,9},{9,8},{10,11... | collective-permute-start | bytes 196616 | tf_op jit(solution)/shard_map/ppermute | solution.py:363
  49.8 5.0 %collective-permute-start = (f32[32,128]{1,0:T(8,128)S(1)}, f32[32,128]{1,0:T(8,128)S(1)}, u32[]{:S(2)}, u32[]{:S(2)}) collective-permute-start(f32[32,128]{1,0:T(8,128)S(1)} %get-tuple-element.19), channel_id=1, source_target_pairs={{0,32},{32,64},{64,96},{96,128},{128,160},{160,192},{192,224},{224... | collective-permute-start | bytes 49160 | tf_op jit(solution)/shard_map/ppermute | solution.py:385
  53.1 6.7 %copy-start.2 = (f32[8,16,128]{2,1,0:T(8,128)S(1)}, f32[8,16,128]{2,1,0:T(8,128)}, u32[]{:S(2)}) copy-start(f32[8,16,128]{2,1,0:T(8,128)} %param.12) | copy-start | bytes 196612
  53.1 6.7 %copy-start.6 = (f32[8,8]{1,0:T(8,128)S(1)}, f32[8,8]{1,0:T(8,128)}, u32[]{:S(2)}) copy-start(f32[8,8]{1,0:T(8,128)} %inv_ref.1) | copy-start | bytes 772
  53.1 6.7 %collective-permute-start.1 = (f32[32,128]{1,0:T(8,128)S(1)}, f32[32,128]{1,0:T(8,128)S(1)}, u32[]{:S(2)}, u32[]{:S(2)}) collective-permute-start(f32[32,128]{1,0:T(8,128)S(1)} %get-tuple-element.20), channel_id=1, source_target_pairs={{32,0},{64,32},{96,64},{128,96},{160,128},{192,160},{224,192},{256... | collective-permute-start | bytes 49160 | tf_op jit(solution)/shard_map/ppermute | solution.py:386
  62.0 25.0 %copy-start.10 = (f32[512]{0:T(512)S(1)}, f32[512]{0:T(512)}, u32[]{:S(2)}) copy-start(f32[512]{0:T(512)} %param.21) | copy-start | bytes 6148
